TPU v7x, 256 devices: a whole 4x4x8 slice. The times are simulated.
256 devices in a mesh: dp: 64 (over z, y, x_hi), mp: 4 (over x_lo, core).
Axes of the slice: x: 4 (x_hi: 2, x_lo: 2; x = x_hi * 2 + x_lo), y: 4, z: 8, core: 2. Of those that a mesh axis runs over, the one named last changes fastest.
Arguments:
- feats: bfloat16 [344064, 512], P('dp', 'mp'), may hold values from -6 to 6
- conv_weight: bfloat16 [1024, 512], P(None, 'mp'), may hold values from -0.1875 to 0.1875
- conv_bias: float32 [512], P('mp'), may hold values from -3 to 3
- norm_gain: float32 [512], P('mp'), may hold values from 0.1 to 1.9
- norm_shift: float32 [512], P('mp'), may hold values from -3 to 3
- lengths: int32 [192], P('dp'), may hold values from 143760 to 287119
- grad_rows: bfloat16 [172032, 512], P('dp', 'mp'), may hold values from -6 to 6
- seg_owner: int32 [1344], P('dp'), may hold values from 0 to 63, as said below
- seg_slot: int32 [1344], P('dp'), may hold values from 0 to 20, as said below
Outputs:
- grad_feats: bfloat16 [344064, 512], P('dp', 'mp')
- grad_weight: float32 [1024, 512], P(None, 'mp')
- grad_bias: float32 [512], P('mp')
- grad_gain: float32 [512], P('mp')
- grad_shift: float32 [512], P('mp')
Inputs may be any that keep to these rules, and one draw needn't show every extreme that they name: `seg_owner`: each index of dp sends its frame blocks to distinct owners exactly 2 at a time (one owner fewer at most); every owner receives exactly 21 blocks, one for each of its slots. `seg_slot`: owner and slot together name every block slot of every owner exactly once.
All inputs are finite; a program needn't handle non-finite values.
Results may differ from a plain program's by a relative error of at most 0.0049.
Values may be sent and summed in bfloat16 or wider, within the bound.
No kernel may reach another device: no remote copies, remote signals or barrier semaphores. Data moves between devices by JAX's collectives and lax.ppermute only.
A program may use at most 128 MiB of HBM per device.

v0:
```python
import math

import jax
import jax.numpy as jnp
import numpy as np
from jax import lax
from jax.experimental import pallas as pl
from jax.experimental.pallas import tpu as pltpu
from jax.sharding import Mesh, PartitionSpec as P

BLOCK = 128
BPU = 7
SLOTS = 21
PAD = 24
DP = 64
LANES = 128
FRAMES = 32

MIB = 1024 * 1024
VMEM = 28 * MIB
ALL_VMEM = 60 * MIB

EPSILON = 1e-05
INV_ROOT_TWO = 0.7071067811865476
INV_ROOT_TAU = 0.3989422804014327


def gelu_slope(value):
    return (
        0.5 * (1.0 + lax.erf(value * INV_ROOT_TWO))
        + value * jnp.exp(-0.5 * value * value) * INV_ROOT_TAU
    )


def swap(value, axis):
    return lax.ppermute(value, axis, [(0, 1), (1, 0)])


def pick(array, index, axis):
    return lax.dynamic_index_in_dim(array, index, axis, keepdims=False)


def ordered(flag, mine, other):
    return jnp.where(flag == 0, mine, other), jnp.where(flag == 0, other, mine)


def lay_out_kernel(
    rows_ref, owner_ref, slot_ref, out_ref, held_ref, owners_ref, slots_ref, wide_ref, sems
):
    copies = [
        pltpu.make_async_copy(rows_ref, held_ref, sems.at[0]),
        pltpu.make_async_copy(owner_ref, owners_ref, sems.at[1]),
        pltpu.make_async_copy(slot_ref, slots_ref, sems.at[2]),
    ]
    for copy in copies:
        copy.start()
    wide_ref[(SLOTS + 2) * BLOCK :] = jnp.zeros((BLOCK, LANES), jnp.float32)
    lane = lax.broadcasted_iota(jnp.int32, (1, LANES), 1)
    for place, label_ref in enumerate((owners_ref, slots_ref)):
        copies[1 + place].wait()
        label = jnp.zeros((1, LANES), jnp.int32)
        for block in range(SLOTS):
            label = jnp.where(lane == block, label_ref[block], label)
        start = (SLOTS + place) * BLOCK
        wide_ref[start : start + BLOCK] = jnp.broadcast_to(
            label.astype(jnp.float32), (BLOCK, LANES)
        )
    copies[0].wait()
    wide_ref[: SLOTS * BLOCK] = held_ref[...].astype(jnp.float32)
    for half in range(2):
        for frame in range(DP):
            column = wide_ref[pl.ds(half * DP + frame, PAD, stride=BLOCK), :]
            out_ref[frame, half] = column.astype(jnp.bfloat16)


def lay_out(grad_rows, seg_owner, seg_slot):
    return pl.pallas_call(
        lay_out_kernel,
        out_shape=jax.ShapeDtypeStruct((DP, 2, PAD, LANES), jnp.bfloat16),
        in_specs=[pl.BlockSpec(memory_space=pl.ANY)] * 3,
        scratch_shapes=[
            pltpu.VMEM((SLOTS * BLOCK, LANES), jnp.bfloat16),
            pltpu.SMEM((SLOTS,), jnp.int32),
            pltpu.SMEM((SLOTS,), jnp.int32),
            pltpu.VMEM((PAD * BLOCK, LANES), jnp.float32),
            pltpu.SemaphoreType.DMA((3,)),
        ],
        compiler_params=pltpu.CompilerParams(vmem_limit_bytes=ALL_VMEM),
        cost_estimate=pl.CostEstimate(flops=0, bytes_accessed=1500000, transcendentals=0),
    )(grad_rows, seg_owner, seg_slot)


def permute_kernel(lane_ref, spread_ref, out_ref, rows_ref, labels_ref, target_ref):
    step = pl.program_id(0)
    owners = out_ref.shape[0]
    tile = owners * PAD
    width = DP * PAD

    @pl.when(step == 0)
    def _():
        for half in range(2):
            values = spread_ref[:, half].astype(jnp.float32).reshape(width, LANES)
            rows_ref[:, half * LANES : (half + 1) * LANES] = values.astype(jnp.bfloat16)
        labels_ref[...] = spread_ref[:, 0, PAD - 8 :].astype(jnp.float32).reshape(DP * 8, LANES)
        block = lane_ref[0:1, :]
        source = lane_ref[1:2, :]
        repeat = jnp.where(
            lax.broadcasted_iota(jnp.int32, (LANES, width), 0) == block, 1.0, 0.0
        ).astype(jnp.bfloat16)
        own_row = lax.broadcasted_iota(jnp.int32, (DP, width), 0) == source
        found = []
        for row in (SLOTS, SLOTS + 1):
            label = labels_ref[pl.ds(row - (PAD - 8), DP, stride=8), :].astype(jnp.bfloat16)
            spun = jnp.dot(label, repeat, preferred_element_type=jnp.float32)
            found.append(jnp.sum(jnp.where(own_row, spun, 0.0), axis=0, keepdims=True))
        target = (found[0] * PAD + found[1]).astype(jnp.int32)
        target_ref[...] = jnp.where(block < SLOTS, target, -1)

    wanted = step * tile + lax.broadcasted_iota(jnp.int32, (tile, DP * PAD), 0)
    choose = jnp.where(target_ref[...] == wanted, 1.0, 0.0).astype(jnp.bfloat16)
    moved = jnp.dot(choose, rows_ref[...], preferred_element_type=jnp.float32)
    for half in range(2):
        values = moved[:, half * LANES : (half + 1) * LANES].reshape(owners, PAD, LANES)
        out_ref[:, half] = values.astype(jnp.bfloat16)


def permute_pieces(spread):
    steps = 4
    width = DP * PAD
    lanes = np.arange(width, dtype=np.int32)
    places = np.concatenate([np.stack([lanes % PAD, lanes // PAD]), np.zeros((6, width), np.int32)])
    return pl.pallas_call(
        permute_kernel,
        grid=(steps,),
        out_shape=jax.ShapeDtypeStruct(spread.shape, jnp.bfloat16),
        in_specs=[
            pl.BlockSpec((8, width), lambda i: (0, 0)),
            pl.BlockSpec(spread.shape, lambda i: (0, 0, 0, 0)),
        ],
        out_specs=pl.BlockSpec((DP // steps, 2, PAD, LANES), lambda i: (i, 0, 0, 0)),
        scratch_shapes=[
            pltpu.VMEM((width, 2 * LANES), jnp.bfloat16),
            pltpu.VMEM((DP * 8, LANES), jnp.float32),
            pltpu.VMEM((1, width), jnp.int32),
        ],
        compiler_params=pltpu.CompilerParams(vmem_limit_bytes=VMEM),
        cost_estimate=pl.CostEstimate(
            flops=4 * 2 * width * width * 2 * LANES, bytes_accessed=1600000, transcendentals=0
        ),
    )(places, spread)


def parameter(terms, which):
    terms = terms.astype(jnp.float32)
    return sum(terms[3 * part + which : 3 * part + which + 1] for part in range(3))


def forward_kernel(
    place_ref, lengths_ref, feats_ref, packed_ref, link_ref, beside_ref,
    transposed_ref, slope_ref, normed_ref, weight_ref, rows_ref, wide_ref,
):
    step = pl.program_id(0)
    link, core = place_ref[0], place_ref[1]
    blocks = SLOTS * 2 * FRAMES
    rows, channels = normed_ref.shape
    frames = rows // PAD

    @pl.when(step == 0)
    def _():
        sources = (
            (link * 2 + core, feats_ref[:, 0].astype(jnp.float32).reshape(blocks, LANES), packed_ref[...]),
            (
                (1 - link) * 2 + core,
                link_ref[pl.ds(pl.multiple_of(core * blocks, 16), blocks), :].astype(jnp.float32),
                link_ref[2 * blocks :],
            ),
            (link * 2 + 1 - core, beside_ref[0, :blocks].astype(jnp.float32), beside_ref[0, blocks:]),
            (
                (1 - link) * 2 + 1 - core,
                beside_ref[1, :blocks].astype(jnp.float32),
                beside_ref[1, blocks:],
            ),
        )
        for place, value, weight in sources:
            rows_ref[place, :blocks] = value
            weight_ref[:, pl.ds(pl.multiple_of(place * LANES, LANES), LANES)] = weight
        rows_ref[:, blocks:] = jnp.zeros((4, (PAD - SLOTS) * 2 * FRAMES, LANES), jnp.float32)

    for frame in range(frames):
        for tap in range(2):
            for piece in range(4):
                start = 2 * (step * frames + frame) + tap
                column = tap * channels + piece * LANES
                wide_ref[frame * PAD : (frame + 1) * PAD, column : column + LANES] = rows_ref[
                    piece, pl.ds(start, PAD, stride=2 * FRAMES), :
                ]
    paired = wide_ref[...].astype(jnp.bfloat16)
    transposed_ref[...] = paired.T
    terms = weight_ref[2 * channels :]
    preact = jnp.dot(paired, weight_ref[: 2 * channels], preferred_element_type=jnp.float32)
    preact = preact + parameter(terms, 0)
    centred = preact - jnp.sum(preact, axis=1, keepdims=True) * (1.0 / channels)
    spread = jnp.sum(centred * centred, axis=1, keepdims=True) * (1.0 / channels)
    inv_spread = lax.rsqrt(spread + EPSILON)
    normed = centred * inv_spread
    slope = gelu_slope(normed * parameter(terms, 1) + parameter(terms, 2))
    slot = lax.broadcasted_iota(jnp.int32, (PAD, 1), 0)
    limit = jnp.zeros((PAD, 1), jnp.int32)
    for index in range(SLOTS):
        valid = lax.div(lengths_ref[index // BPU] - 400, 320) + 1
        here = valid - (index % BPU) * BLOCK - (link * 2 + core) * FRAMES
        limit = jnp.where(slot == index, here, limit)
    limits = jnp.concatenate([limit - frame for frame in range(frames)], axis=0)
    slope_ref[:, :channels] = jnp.where(limits > step * frames, slope, 0.0)
    slope_ref[:, channels:] = jnp.broadcast_to(inv_spread, (rows, LANES))
    normed_ref[...] = normed


def forward(link, core, lengths, feats, packed, from_link, from_core):
    steps = 2
    rows = FRAMES * PAD
    channels = 4 * LANES
    tile = rows // steps
    return pl.pallas_call(
        forward_kernel,
        grid_spec=pltpu.PrefetchScalarGridSpec(
            num_scalar_prefetch=2,
            grid=(steps,),
            in_specs=[
                pl.BlockSpec(
                    (SLOTS, 1, 2 * FRAMES, LANES),
                    lambda i, place, _: (0, 2 * place[0] + place[1], 0, 0),
                ),
                pl.BlockSpec(packed.shape, lambda i, place, _: (0, 0)),
                pl.BlockSpec(from_link.shape, lambda i, place, _: (0, 0)),
                pl.BlockSpec(from_core.shape, lambda i, place, _: (0, 0, 0)),
            ],
            out_specs=(
                pl.BlockSpec((2 * channels, tile), lambda i, place, _: (0, i)),
                pl.BlockSpec((tile, channels + LANES), lambda i, place, _: (i, 0)),
                pl.BlockSpec((tile, channels), lambda i, place, _: (i, 0)),
                pl.BlockSpec((packed.shape[0], channels), lambda i, place, _: (0, 0)),
            ),
            scratch_shapes=[
                pltpu.VMEM((4, PAD * 2 * FRAMES, LANES), jnp.float32),
                pltpu.VMEM((tile, 2 * channels), jnp.float32),
            ],
        ),
        out_shape=(
            pltpu.HBM((2 * channels, rows), jnp.bfloat16),
            pltpu.HBM((rows, channels + LANES), jnp.float32),
            pltpu.HBM((rows, channels), jnp.float32),
            jax.ShapeDtypeStruct((packed.shape[0], channels), jnp.bfloat16),
        ),
        compiler_params=pltpu.CompilerParams(vmem_limit_bytes=VMEM),
        cost_estimate=pl.CostEstimate(
            flops=3 * 4 * rows * channels * channels,
            bytes_accessed=8000000,
            transcendentals=2 * rows * channels,
        ),
    )(jnp.stack([link, core]), lengths, feats, packed, from_link, from_core)


def backward_kernel(
    core_ref, own_ref, other_ref, slope_ref, normed_ref, gain_ref, transposed_ref,
    low_ref, keep_ref, send_ref, sums_ref, paired_ref, sem,
):
    step = pl.program_id(0)
    fetch = pltpu.make_async_copy(transposed_ref, paired_ref, sem)

    @pl.when(step == 0)
    def _():
        fetch.start()

    rows = slope_ref.shape[0]
    first = core_ref[0] == 0
    columns = []
    for link in range(2):
        own = own_ref[0, :, link].astype(jnp.float32).reshape(rows, LANES)
        other = other_ref[:, link].astype(jnp.float32).reshape(rows, LANES)
        columns.append(jnp.where(first, own, other))
        columns.append(jnp.where(first, other, own))
    upstream = jnp.concatenate(columns, axis=1)
    normed = normed_ref[...]
    channels = normed.shape[1]
    grad_act = upstream * slope_ref[:, :channels]
    weighted = grad_act * normed
    gain = parameter(gain_ref[...], 1)
    grad_normed = grad_act * gain
    grad_mean = jnp.sum(grad_normed, axis=1, keepdims=True) * (1.0 / channels)
    cross_mean = jnp.sum(weighted * gain, axis=1, keepdims=True) * (1.0 / channels)
    grad_pre = slope_ref[:, channels : channels + 1] * (grad_normed - grad_mean - normed * cross_mean)
    low_ref[pl.ds(pl.multiple_of(step * rows, 16), rows), :] = grad_pre.astype(jnp.bfloat16)
    sums = jnp.concatenate(
        [
            jnp.sum(grad_pre, axis=0, keepdims=True),
            jnp.sum(weighted, axis=0, keepdims=True),
            jnp.sum(grad_act, axis=0, keepdims=True),
            jnp.zeros((5, channels), jnp.float32),
        ],
        axis=0,
    )

    @pl.when(step == 0)
    def _():
        sums_ref[...] = sums

    @pl.when(step > 0)
    def _():
        sums_ref[...] += sums

    @pl.when(step == pl.num_programs(0) - 1)
    def _():
        fetch.wait()
        depth = paired_ref.shape[0]
        for target_ref, which in ((send_ref, 1 - core_ref[0]), (keep_ref, core_ref[0])):
            places = [pl.ds(pl.multiple_of((2 * link + which) * LANES, LANES), LANES) for link in range(2)]
            columns = jnp.concatenate([low_ref[:, place] for place in places], axis=1)
            product = jnp.dot(paired_ref[...], columns, preferred_element_type=jnp.float32)
            for link in range(2):
                target_ref[link, :depth] = product[:, link * LANES : (link + 1) * LANES]
                target_ref[link, depth:] = sums_ref[:, places[link]]


def backward(core, own, other, slope, normed, gain, transposed):
    steps = 4
    rows, channels = normed.shape
    depth = transposed.shape[0]
    tile = rows // steps
    frames = FRAMES // steps
    half = jax.ShapeDtypeStruct((2, depth + 8, LANES), jnp.float32)
    return pl.pallas_call(
        backward_kernel,
        grid_spec=pltpu.PrefetchScalarGridSpec(
            num_scalar_prefetch=1,
            grid=(steps,),
            in_specs=[
                pl.BlockSpec((1, frames, 2, PAD, LANES), lambda i, core: (core[0], i, 0, 0, 0)),
                pl.BlockSpec((frames, 2, PAD, LANES), lambda i, core: (i, 0, 0, 0)),
                pl.BlockSpec((tile, channels + LANES), lambda i, core: (i, 0)),
                pl.BlockSpec((tile, channels), lambda i, core: (i, 0)),
                pl.BlockSpec((16, channels), lambda i, core: (depth // 16, 0)),
                pl.BlockSpec(memory_space=pl.ANY),
            ],
            out_specs=(
                pl.BlockSpec((rows, channels), lambda i, core: (0, 0)),
                pl.BlockSpec(half.shape, lambda i, core: (0, 0, 0)),
                pl.BlockSpec(half.shape, lambda i, core: (0, 0, 0)),
            ),
            scratch_shapes=[
                pltpu.VMEM((8, channels), jnp.float32),
                pltpu.VMEM((depth, rows), jnp.bfloat16),
                pltpu.SemaphoreType.DMA,
            ],
        ),
        out_shape=(jax.ShapeDtypeStruct((rows, channels), jnp.bfloat16), half, half),
        compiler_params=pltpu.CompilerParams(vmem_limit_bytes=48 * MIB),
        cost_estimate=pl.CostEstimate(
            flops=2 * rows * depth * channels, bytes_accessed=9000000, transcendentals=0
        ),
    )(core.reshape(1), own, other, slope, normed, gain, transposed)


def input_kernel(core_ref, low_ref, weight_ref, keep_ref, send_ref):
    low = low_ref[...]
    for target_ref, which in ((send_ref, 1 - core_ref[0]), (keep_ref, core_ref[0])):
        for tap in range(2):
            rows = [
                weight_ref[pl.ds(pl.multiple_of((4 * tap + 2 * link + which) * LANES, LANES), LANES), :]
                for link in range(2)
            ]
            product = lax.dot_general(
                low, jnp.concatenate(rows, axis=0), (((1,), (1,)), ((), ())),
                preferred_element_type=jnp.float32,
            ).astype(jnp.bfloat16)
            for link in range(2):
                target_ref[link, tap] = product[:, link * LANES : (link + 1) * LANES]


def input_gradient(core, low, weight):
    rows = low.shape[0]
    half = jax.ShapeDtypeStruct((2, 2, rows, LANES), jnp.bfloat16)
    return pl.pallas_call(
        input_kernel,
        out_shape=(half, half),
        in_specs=[
            pl.BlockSpec(memory_space=pltpu.SMEM),
            pl.BlockSpec(memory_space=pltpu.VMEM),
            pl.BlockSpec(memory_space=pltpu.VMEM),
        ],
        out_specs=(pl.BlockSpec(memory_space=pltpu.VMEM),) * 2,
        compiler_params=pltpu.CompilerParams(vmem_limit_bytes=VMEM),
        cost_estimate=pl.CostEstimate(
            flops=4 * rows * weight.shape[1] * weight.shape[1],
            bytes_accessed=3500000,
            transcendentals=0,
        ),
    )(core.reshape(1), low, weight)


def chip_kernel(keep_ref, other_ref, weight_ref, vector_ref):
    total = keep_ref[0] + other_ref[0]
    depth = total.shape[0] - 8
    weight_ref[:, 0] = total[:depth].reshape(DP, depth // DP, LANES).astype(jnp.bfloat16)
    vector_ref[0] = total[depth:]


def chip_total(keep, other):
    depth = keep.shape[1] - 8
    return pl.pallas_call(
        chip_kernel,
        grid=(2,),
        out_shape=(
            jax.ShapeDtypeStruct((DP, 2, depth // DP, LANES), jnp.bfloat16),
            jax.ShapeDtypeStruct((2, 8, LANES), jnp.float32),
        ),
        in_specs=[pl.BlockSpec((1, depth + 8, LANES), lambda i: (i, 0, 0))] * 2,
        out_specs=(
            pl.BlockSpec((DP, 1, depth // DP, LANES), lambda i: (0, i, 0, 0)),
            pl.BlockSpec((1, 8, LANES), lambda i: (i, 0, 0)),
        ),
        compiler_params=pltpu.CompilerParams(vmem_limit_bytes=VMEM),
        cost_estimate=pl.CostEstimate(
            flops=2 * depth * LANES, bytes_accessed=2700000, transcendentals=0
        ),
    )(keep, other)


def route(grad_rows, seg_owner, seg_slot):
    outgoing = lay_out(grad_rows, seg_owner, seg_slot)
    spread = lax.all_to_all(outgoing, "dp", split_axis=0, concat_axis=0, tiled=True)
    sorted_pieces = permute_pieces(spread).reshape(2 * DP, PAD, LANES)
    arrived = lax.all_to_all(
        sorted_pieces, ("dp", "l"), split_axis=0, concat_axis=0, tiled=True
    ).reshape(2, FRAMES, 2, PAD, LANES)
    return arrived, sorted_pieces


def pack_parameters(conv_weight, vectors):
    high = lax.reduce_precision(vectors, 8, 7)
    middle = lax.reduce_precision(vectors - high, 8, 7)
    terms = jnp.concatenate([high, middle, vectors - high - middle]).astype(jnp.bfloat16)
    return jnp.concatenate([conv_weight, jnp.pad(terms, ((0, 7), (0, 0)))], axis=0)


def on_device(
    feats, conv_weight, conv_bias, norm_gain, norm_shift, lengths, grad_rows, seg_owner, seg_slot
):
    link, core = lax.axis_index("l"), lax.axis_index("c")
    channels = 4 * LANES

    own, sorted_pieces = route(grad_rows, seg_owner, seg_slot)

    packed = pack_parameters(conv_weight, jnp.stack([conv_bias, norm_gain, norm_shift]))
    by_group = feats.reshape(SLOTS, 2, 2, 2 * FRAMES, LANES).transpose(1, 2, 0, 3, 4)
    by_group = by_group.reshape(2, 2, SLOTS * 2 * FRAMES, LANES)
    away = pick(by_group, 1 - link, 0)
    from_link = swap(jnp.concatenate([away.reshape(-1, LANES), packed]), "l")
    from_link, _ = lax.optimization_barrier((from_link, sorted_pieces))
    rows = SLOTS * 2 * FRAMES
    beside = jnp.stack(
        [
            jnp.concatenate([pick(pick(by_group, link, 0), 1 - core, 0), packed]),
            jnp.concatenate(
                [
                    lax.dynamic_slice_in_dim(from_link, (1 - core) * rows, rows),
                    from_link[2 * rows :],
                ]
            ),
        ]
    )
    from_core = swap(beside, "c")
    transposed, slope, normed, weight = forward(
        link, core, lengths, feats.reshape(SLOTS, 4, 2 * FRAMES, LANES), packed, from_link, from_core
    )

    leaving, _ = lax.optimization_barrier((pick(own, 1 - core, 0), normed))
    other = swap(leaving, "c")

    low, keep, send = backward(
        core, own, other, slope, normed, weight, transposed
    )
    chip_weight, chip_vector = chip_total(keep, swap(send, "c"))

    scale = 1.0 / math.sqrt(DP * SLOTS * BLOCK)
    group_vector = pick(chip_vector, link, 0) + swap(pick(chip_vector, 1 - link, 0), "l")
    terms = lax.all_to_all(
        chip_weight.reshape(2 * DP, 16, LANES), ("dp", "l"), split_axis=0, concat_axis=0, tiled=True
    )
    total = (jnp.sum(terms.astype(jnp.float32), axis=0) * scale).astype(jnp.bfloat16)
    high = lax.reduce_precision(group_vector[:3], 8, 7)
    rest = group_vector[:3] - high
    pair = jnp.concatenate([high, rest]).astype(jnp.bfloat16)
    announce = jnp.concatenate([total, pair, jnp.zeros((2, LANES), jnp.bfloat16)], axis=0)
    heard = lax.all_to_all(
        jnp.broadcast_to(announce, (DP, PAD, LANES)), "dp", split_axis=0, concat_axis=0, tiled=True
    )
    weight_out = heard[:, :16].reshape(2 * channels, LANES).astype(jnp.float32)
    sums = jnp.sum(heard[:, 16:22].astype(jnp.float32), axis=0)
    vector_out = (sums[:3] + sums[3:]) * scale

    own_rows, leaving_rows = input_gradient(core, low, weight)
    chip_rows = jnp.stack([own_rows, swap(leaving_rows, "c")])
    here = pick(chip_rows, link, 1)
    there = swap(pick(chip_rows, 1 - link, 1), "l")
    groups = []
    for part in (0, 1):
        rows = jnp.where(link == part, here, there)
        groups.extend(ordered(core, rows[0], rows[1]))
    grad_feats = (
        jnp.stack(groups)
        .reshape(4, 2, FRAMES, PAD, LANES)[:, :, :, :SLOTS]
        .transpose(3, 0, 2, 1, 4)
        .reshape(feats.shape)
    )
    return (grad_feats, weight_out, vector_out[0], vector_out[1], vector_out[2])


def solution(mesh):
    grid = Mesh(mesh.devices.reshape(DP, 2, 2), ("dp", "l", "c"))
    mp = ("l", "c")
    placed = (
        P("dp", mp),
        P(None, mp),
        P(mp),
        P(mp),
        P(mp),
        P("dp"),
        P("dp", mp),
        P("dp"),
        P("dp"),
    )
    return jax.shard_map(
        on_device,
        mesh=grid,
        in_specs=placed,
        out_specs=(P("dp", mp), P(None, mp), P(mp), P(mp), P(mp)),
        check_vma=False,
    )
```

profile of v0, /device:TPU:2, one launch (start us, length us, event | category | flops | bytes accessed | tf_op | source)
XLA Modules:
  0.0 138.6 jit_solution(1884059072175970727)
XLA Ops:
  0.6 0.0 copy-start
  0.6 3.1 %shard_map.137 = bf16[64,2,24,128]{3,2,1,0:T(8,128)(2,1)} custom-call(bf16[2688,128]{1,0:T(8,128)(2,1)} %rows_ref.1, s32[21]{0:T(128)} %owner_ref.1, s32[21]{0:T(128)} %slot_ref.1), custom_call_target="tpu_custom_call" | custom-call | bytes 1500000 | tf_op jit(solution)/shard_map/pallas_call | solution.py:77
  3.7 13.7 %all-to-all-start = ((bf16[64,2,24,128]{3,2,1,0:T(8,128)(2,1)}), bf16[64,2,24,128]{3,2,1,0:T(8,128)(2,1)S(1)}, u32[]{:S(2)}, u32[]{:S(2)}) async-start(bf16[64,2,24,128]{3,2,1,0:T(8,128)(2,1)} %shard_map.137), calls=%async_computation | async-start | bytes 1572864 | tf_op jit(solution)/shard_map/all_to_all | solution.py:431
  17.4 0.0 copy-start.9
  17.4 0.0 copy-start.10
  17.4 0.0 copy-start.11
  17.5 0.1 copy.17
  17.6 0.0 copy-start.5
  17.6 0.0 copy-start.7
  17.6 0.4 copy-done.9
  18.1 0.0 copy-done.10
  18.1 0.0 copy-done.11
  18.1 0.1 constant_dynamic-slice_fusion.1
  18.2 0.5 copy-done.5
  18.7 0.1 copy-done.7
  18.8 1.0 pad_maximum_fusion.4
  19.8 1.4 %collective-permute-start = (bf16[3728,128]{1,0:T(8,128)(2,1)}, bf16[3728,128]{1,0:T(8,128)(2,1)S(1)}, u32[]{:S(2)}, u32[]{:S(2)}) collective-permute-start(bf16[3728,128]{1,0:T(8,128)(2,1)} %pad_maximum_fusion.4), channel_id=1, source_target_pairs={{0,2},{2,0},{1,3},{3,1},{4,6},{6,4},{5,7},{7,5},{8,10},{10,8},{9,1... | collective-permute-start | bytes 2863112 | tf_op jit(solution)/shard_map/ppermute | solution.py:36
  21.2 1.0 dynamic-slice_bitcast_fusion.1
  22.2 0.9 maximum_bitcast_fusion
  23.1 18.9 %all-to-all-done.spread_ref = bf16[64,2,24,128]{3,2,1,0:T(8,128)(2,1)S(1)} async-done(((bf16[64,2,24,128]{3,2,1,0:T(8,128)(2,1)}), bf16[64,2,24,128]{3,2,1,0:T(8,128)(2,1)S(1)}, u32[]{:S(2)}, u32[]{:S(2)}) %all-to-all-start) | async-done | bytes 786464 | tf_op jit(solution)/shard_map/all_to_all | solution.py:431
  42.0 3.3 %shard_map.138 = bf16[64,2,24,128]{3,2,1,0:T(8,128)(2,1)} custom-call(s32[8,1536]{1,0:T(8,128)S(1)} %copy-done.4, bf16[64,2,24,128]{3,2,1,0:T(8,128)(2,1)S(1)} %all-to-all-done.spread_ref), custom_call_target="tpu_custom_call" | custom-call | flops 4831838208 | bytes 1600000 | tf_op jit(solution)/shard_map/pallas_call | solution.py:132
  45.3 7.9 %all-to-all-start.1 = ((bf16[128,24,128]{2,1,0:T(8,128)(2,1)}), bf16[128,24,128]{2,1,0:T(8,128)(2,1)S(1)}, u32[]{:S(2)}, u32[]{:S(2)}) async-start(bf16[128,24,128]{2,1,0:T(8,128)(2,1)} %bitcast.1), calls=%async_computation.1 | async-start | bytes 1572864 | tf_op jit(solution)/shard_map/all_to_all | solution.py:433
  53.1 0.0 copy-start.6
  53.1 0.0 collective-permute-done.link_ref
  53.1 0.0 copy-start.1
  53.3 1.3 copy-done.6
  54.5 0.1 pad_maximum_fusion.3
  54.7 0.0 copy-done.1
  54.7 0.1 collective-permute-start.1
  54.8 0.1 pad_add_fusion.place_ref
  54.9 2.8 %collective-permute-done.1.beside_ref = bf16[2,2384,128]{2,1,0:T(8,128)(2,1)S(1)} collective-permute-done((bf16[2,2384,128]{2,1,0:T(8,128)(2,1)S(1)}, bf16[2,2384,128]{2,1,0:T(8,128)(2,1)S(1)}, u32[]{:S(2)}, u32[]{:S(2)}) %collective-permute-start.1) | collective-permute-done | bytes 1220640 | tf_op jit(solution)/shard_map/ppermute | solution.py:36
  57.7 0.0 copy-done.3
  57.7 1.2 copy-done.2
  58.9 5.7 %shard_map.139 = (bf16[1024,768]{1,0:T(8,128)(2,1)}, f32[768,640]{1,0:T(8,128)}, f32[768,512]{1,0:T(8,128)}, bf16[1040,512]{1,0:T(8,128)(2,1)S(1)}) custom-call(s32[2]{0:T(128)S(1)} %pad_add_fusion.place_ref, s32[3]{0:T(128)S(1)} %copy-done.3, bf16[21,4,64,128]{3,2,1,0:T(8,128)(2,1)S(1)} %bitcast.57, bf16[1040,128]{1,0:T(8,128)(2,1)S(1)} %pad_maximum_fusion.5.packed_ref, ...), custom_call_target="tpu_custom_call" | custom-call | flops 2415919104 | bytes 8000000 | tf_op jit(solution)/shard_map/pallas_call | solution.py:224
  64.5 13.0 %all-to-all-done.1 = bf16[128,24,128]{2,1,0:T(8,128)(2,1)S(1)} async-done(((bf16[128,24,128]{2,1,0:T(8,128)(2,1)}), bf16[128,24,128]{2,1,0:T(8,128)(2,1)S(1)}, u32[]{:S(2)}, u32[]{:S(2)}) %all-to-all-start.1) | async-done | bytes 786464 | tf_op jit(solution)/shard_map/all_to_all | solution.py:433
  77.6 0.1 collective-permute-start.2
  77.7 1.7 %collective-permute-done.2.other_ref = bf16[32,2,24,128]{3,2,1,0:T(8,128)(2,1)S(1)} collective-permute-done((bf16[32,2,24,128]{3,2,1,0:T(8,128)(2,1)S(1)}, bf16[32,2,24,128]{3,2,1,0:T(8,128)(2,1)S(1)}, u32[]{:S(2)}, u32[]{:S(2)}) %collective-permute-start.2) | collective-permute-done | bytes 393248 | tf_op jit(solution)/shard_map/ppermute | solution.py:36
  79.4 4.6 %shard_map.140 = (bf16[768,512]{1,0:T(8,128)(2,1)S(1)}, f32[2,1032,128]{2,1,0:T(8,128)S(1)}, f32[2,1032,128]{2,1,0:T(8,128)S(1)}) custom-call(s32[1]{0:T(128)} %bitcast.core_ref, bf16[2,32,2,24,128]{4,3,2,1,0:T(8,128)(2,1)S(1)} %bitcast.53, bf16[32,2,24,128]{3,2,1,0:T(8,128)(2,1)S(1)} %collective-permute-done.2.other_ref, ...), custom_call_target="tpu_custom_call" | custom-call | flops 805306368 | bytes 9000000 | tf_op jit(solution)/shard_map/pallas_call | solution.py:332
  84.0 0.2 collective-permute-start.5
  84.3 1.0 shard_map.141
  85.3 0.7 collective-permute-start.3
  85.9 0.9 collective-permute-done.5.other_ref
  86.8 0.9 shard_map.142
  87.7 6.9 %all-to-all-start.2 = ((bf16[128,16,128]{2,1,0:T(8,128)(2,1)}), bf16[128,16,128]{2,1,0:T(8,128)(2,1)S(1)}, u32[]{:S(2)}, u32[]{:S(2)}) async-start(bf16[128,16,128]{2,1,0:T(8,128)(2,1)} %bitcast.26), calls=%async_computation.2 | async-start | bytes 1048576 | tf_op jit(solution)/shard_map/all_to_all | solution.py:487
  94.6 0.1 pad.8.clone
  94.7 1.0 collective-permute-start.6
  95.8 0.0 collective-permute-done.3
  95.8 1.0 fusion.2
  96.7 1.0 collective-permute-start.4
  97.7 0.7 collective-permute-done.6
  98.5 16.9 %all-to-all-done.2 = bf16[128,16,128]{2,1,0:T(8,128)(2,1)S(1)} async-done(((bf16[128,16,128]{2,1,0:T(8,128)(2,1)}), bf16[128,16,128]{2,1,0:T(8,128)(2,1)S(1)}, u32[]{:S(2)}, u32[]{:S(2)}) %all-to-all-start.2) | async-done | bytes 524320 | tf_op jit(solution)/shard_map/all_to_all | solution.py:487
  115.4 0.1 convert_reduce_fusion
  115.5 0.1 maximum_maximum_fusion
  115.6 0.8 broadcast_in_dim.7
  116.4 4.6 %all-to-all-start.3 = ((bf16[64,24,128]{2,1,0:T(8,128)(2,1)}), bf16[64,24,128]{2,1,0:T(8,128)(2,1)S(1)}, u32[]{:S(2)}, u32[]{:S(2)}) async-start(bf16[64,24,128]{2,1,0:T(8,128)(2,1)} %broadcast_in_dim.7), calls=%async_computation.3 | async-start | bytes 786432 | tf_op jit(solution)/shard_map/all_to_all | solution.py:495
  121.0 0.0 collective-permute-done.4
  121.0 1.2 broadcast_select_fusion.1
  122.3 0.1 broadcast_select_fusion.3
  122.4 0.3 fusion
  122.7 2.5 %copy.18 = bf16[21,4,32,2,128]{4,3,2,1,0:T(2,128)(2,1)} copy(bf16[21,4,32,2,128]{4,0,2,3,1:T(8,128)(2,1)S(1)} %fusion) | data formatting | bytes 2752512 | tf_op jit(solution)/shard_map/transpose | solution.py:513
  125.2 12.0 %all-to-all-done.3 = bf16[64,24,128]{2,1,0:T(8,128)(2,1)S(1)} async-done(((bf16[64,24,128]{2,1,0:T(8,128)(2,1)}), bf16[64,24,128]{2,1,0:T(8,128)(2,1)S(1)}, u32[]{:S(2)}, u32[]{:S(2)}) %all-to-all-start.3) | async-done | bytes 393248 | tf_op jit(solution)/shard_map/all_to_all | solution.py:495
  137.2 0.8 bitcast_convert_fusion
  138.0 0.1 convert_reduce_fusion.1
  138.1 0.5 slice_bitcast_fusion
  (21 shorter events, 0.2 us)
Async XLA Ops:
  0.6 16.8 %copy-start = (bf16[5376,128]{1,0:T(8,128)(2,1)S(1)}, bf16[5376,128]{1,0:T(8,128)(2,1)}, u32[]{:S(2)}) copy-start(bf16[5376,128]{1,0:T(8,128)(2,1)} %param.10) | copy-start | bytes 4128772
  3.7 38.2 %all-to-all-start = ((bf16[64,2,24,128]{3,2,1,0:T(8,128)(2,1)}), bf16[64,2,24,128]{3,2,1,0:T(8,128)(2,1)S(1)}, u32[]{:S(2)}, u32[]{:S(2)}) async-start(bf16[64,2,24,128]{3,2,1,0:T(8,128)(2,1)} %shard_map.137), calls=%async_computation | async-start | bytes 1572864 | tf_op jit(solution)/shard_map/all_to_all | solution.py:431
  17.4 0.7 copy-start.9
  17.4 0.7 copy-start.10
  17.4 0.7 copy-start.11
  17.6 1.1 copy-start.5
  17.6 1.1 copy-start.7
  18.8 3.5 %copy-start.8 = (bf16[1024,128]{1,0:T(8,128)(2,1)S(1)}, bf16[1024,128]{1,0:T(8,128)(2,1)}, u32[]{:S(2)}) copy-start(bf16[1024,128]{1,0:T(8,128)(2,1)} %param.11) | copy-start | bytes 786436
  18.8 23.2 %copy-start.4 = (s32[8,1536]{1,0:T(8,128)S(1)}, s32[8,1536]{1,0:T(8,128)}, u32[]{:S(2)}) copy-start(s32[8,1536]{1,0:T(8,128)} %constant.74.clone.lane_ref) | copy-start | bytes 147460
  19.8 33.4 %collective-permute-start = (bf16[3728,128]{1,0:T(8,128)(2,1)}, bf16[3728,128]{1,0:T(8,128)(2,1)S(1)}, u32[]{:S(2)}, u32[]{:S(2)}) collective-permute-start(bf16[3728,128]{1,0:T(8,128)(2,1)} %pad_maximum_fusion.4), channel_id=1, source_target_pairs={{0,2},{2,0},{1,3},{3,1},{4,6},{6,4},{5,7},{7,5},{8,10},{10,8},{9,1... | collective-permute-start | bytes 2863112 | tf_op jit(solution)/shard_map/ppermute | solution.py:36
  45.3 32.3 %all-to-all-start.1 = ((bf16[128,24,128]{2,1,0:T(8,128)(2,1)}), bf16[128,24,128]{2,1,0:T(8,128)(2,1)S(1)}, u32[]{:S(2)}, u32[]{:S(2)}) async-start(bf16[128,24,128]{2,1,0:T(8,128)(2,1)} %bitcast.1), calls=%async_computation.1 | async-start | bytes 1572864 | tf_op jit(solution)/shard_map/all_to_all | solution.py:433
  53.1 1.4 %copy-start.6 = (bf16[1,2384,128]{2,1,0:T(8,128)(2,1)S(1)}, bf16[1,2384,128]{2,1,0:T(8,128)(2,1)}, u32[]{:S(2)}) copy-start(bf16[1,2384,128]{2,1,0:T(8,128)(2,1)} %maximum_bitcast_fusion) | copy-start | bytes 1830916
  53.1 1.5 %copy-start.1 = (bf16[3728,128]{1,0:T(8,128)(2,1)}, bf16[3728,128]{1,0:T(8,128)(2,1)S(1)}, u32[]{:S(2)}) copy-start(bf16[3728,128]{1,0:T(8,128)(2,1)S(1)} %collective-permute-done.link_ref) | copy-start | bytes 2863108
  54.5 3.1 %copy-start.3 = (s32[3]{0:T(128)S(1)}, s32[3]{0:T(128)}, u32[]{:S(2)}) copy-start(s32[3]{0:T(128)} %lengths_ref.1) | copy-start | bytes 40
  54.7 3.0 %collective-permute-start.1 = (bf16[2,2384,128]{2,1,0:T(8,128)(2,1)S(1)}, bf16[2,2384,128]{2,1,0:T(8,128)(2,1)S(1)}, u32[]{:S(2)}, u32[]{:S(2)}) collective-permute-start(bf16[2,2384,128]{2,1,0:T(8,128)(2,1)S(1)} %pad_maximum_fusion.3), channel_id=1, source_target_pairs={{0,1},{1,0},{2,3},{3,2},{4,5},{5,4},{6,7},{7,6},{8,9},{9,8},{10,11... | collective-permute-start | bytes 3661832 | tf_op jit(solution)/shard_map/ppermute | solution.py:36
  57.7 1.2 copy-start.2
  77.6 1.8 %collective-permute-start.2 = (bf16[32,2,24,128]{3,2,1,0:T(8,128)(2,1)S(1)}, bf16[32,2,24,128]{3,2,1,0:T(8,128)(2,1)S(1)}, u32[]{:S(2)}, u32[]{:S(2)}) collective-permute-start(bf16[32,2,24,128]{3,2,1,0:T(8,128)(2,1)S(1)} %dynamic-slice_bitcast_fusion), channel_id=1, source_target_pairs={{0,1},{1,0},{2,3},{3,2},{4,5},{5,4},{6,7},{7,6},{8,9},{9,8},{10,11... | collective-permute-start | bytes 1179656 | tf_op jit(solution)/shard_map/ppermute | solution.py:36
  84.0 2.8 %collective-permute-start.5 = (f32[2,1032,128]{2,1,0:T(8,128)S(1)}, f32[2,1032,128]{2,1,0:T(8,128)S(1)}, u32[]{:S(2)}, u32[]{:S(2)}) collective-permute-start(f32[2,1032,128]{2,1,0:T(8,128)S(1)} %get-tuple-element.28), channel_id=1, source_target_pairs={{0,1},{1,0},{2,3},{3,2},{4,5},{5,4},{6,7},{7,6},{8,9},{9,8},{10,11... | collective-permute-start | bytes 3170312 | tf_op jit(solution)/shard_map/ppermute | solution.py:36
  85.3 10.5 %collective-permute-start.3 = (bf16[2,2,768,128]{3,2,1,0:T(8,128)(2,1)S(1)}, bf16[2,2,768,128]{3,2,1,0:T(8,128)(2,1)S(1)}, u32[]{:S(2)}, u32[]{:S(2)}) collective-permute-start(bf16[2,2,768,128]{3,2,1,0:T(8,128)(2,1)S(1)} %get-tuple-element.26), channel_id=1, source_target_pairs={{0,1},{1,0},{2,3},{3,2},{4,5},{5,4},{6,7},{7,6},{8,9},{9,8},{10,11... | collective-permute-start | bytes 2359304 | tf_op jit(solution)/shard_map/ppermute | solution.py:36
  87.7 27.6 %all-to-all-start.2 = ((bf16[128,16,128]{2,1,0:T(8,128)(2,1)}), bf16[128,16,128]{2,1,0:T(8,128)(2,1)S(1)}, u32[]{:S(2)}, u32[]{:S(2)}) async-start(bf16[128,16,128]{2,1,0:T(8,128)(2,1)} %bitcast.26), calls=%async_computation.2 | async-start | bytes 1048576 | tf_op jit(solution)/shard_map/all_to_all | solution.py:487
  94.7 3.7 %collective-permute-start.6 = (f32[8,128]{1,0:T(8,128)S(1)}, f32[8,128]{1,0:T(8,128)S(1)}, u32[]{:S(2)}, u32[]{:S(2)}) collective-permute-start(f32[8,128]{1,0:T(8,128)S(1)} %dynamic-slice_bitcast_fusion.2), channel_id=1, source_target_pairs={{0,2},{2,0},{1,3},{3,1},{4,6},{6,4},{5,7},{7,5},{8,10},{10,8},{9,1... | collective-permute-start | bytes 12296 | tf_op jit(solution)/shard_map/ppermute | solution.py:36
  96.7 24.3 %collective-permute-start.4 = (bf16[2,2,768,128]{3,2,1,0:T(8,128)(2,1)}, bf16[2,2,768,128]{3,2,1,0:T(8,128)(2,1)}, u32[]{:S(2)}, u32[]{:S(2)}) collective-permute-start(bf16[2,2,768,128]{3,2,1,0:T(8,128)(2,1)} %fusion.2), channel_id=1, source_target_pairs={{0,2},{2,0},{1,3},{3,1},{4,6},{6,4},{5,7},{7,5},{8,10},{10,8},{9,1... | collective-permute-start | bytes 2359304 | tf_op jit(solution)/shard_map/ppermute | solution.py:36
  116.4 20.8 %all-to-all-start.3 = ((bf16[64,24,128]{2,1,0:T(8,128)(2,1)}), bf16[64,24,128]{2,1,0:T(8,128)(2,1)S(1)}, u32[]{:S(2)}, u32[]{:S(2)}) async-start(bf16[64,24,128]{2,1,0:T(8,128)(2,1)} %broadcast_in_dim.7), calls=%async_computation.3 | async-start | bytes 786432 | tf_op jit(solution)/shard_map/all_to_all | solution.py:495
where the time goes:
time: 139 us
  waiting for transfers between devices  66.8 us (48%)
  starting transfers between devices  37.6 us (27%)
  Pallas kernels  18.5 us (13%)
  local copies, waits for them, and re-layouts  8.76 us (6%)
  other arithmetic  5.91 us (4%)
    all_to_all x1, waiting for transfers between devices, route(): lax.all_to_all(outgoing, 'dp', split_axis=0, concat_axis=0, tiled=True)  18.9 us
    all_to_all x1, waiting for transfers between devices, on_device(): lax.all_to_all(chip_weight.reshape(2 * DP, 16, LANES), ('dp', 'l'), split...  16.9 us
    all_to_all x1, starting transfers between devices, route(): lax.all_to_all(outgoing, 'dp', split_axis=0, concat_axis=0, tiled=True)  13.7 us
    all_to_all x1, waiting for transfers between devices, route(): lax.all_to_all(sorted_pieces, ('dp', 'l'), split_axis=0, concat_axis=0, t...  13 us
    all_to_all x1, waiting for transfers between devices, on_device(): lax.all_to_all(jnp.broadcast_to(announce, (DP, PAD, LANES)), 'dp', split_...  12 us
    all_to_all x1, starting transfers between devices, route(): lax.all_to_all(sorted_pieces, ('dp', 'l'), split_axis=0, concat_axis=0, t...  7.86 us
    all_to_all x1, starting transfers between devices, on_device(): lax.all_to_all(chip_weight.reshape(2 * DP, 16, LANES), ('dp', 'l'), split...  6.91 us
    ppermute x7, waiting for transfers between devices, swap(): return lax.ppermute(value, axis, [(0, 1), (1, 0)])  6.09 us
  transfers between devices with their start and end apart: 11, of which 8 were waited for; matrix products, arithmetic and copies ran while one was open for 7% of the time, Pallas kernels for 8%

commit v1 on v0

--- a/solution.py
+++ b/solution.py
@@ -14,6 +14,7 @@
 PAD = 24
 DP = 64
 LANES = 128
+STEPS = 2
 FRAMES = 32
 
 MIB = 1024 * 1024
@@ -125,7 +126,7 @@
 
 
 def permute_pieces(spread):
-    steps = 4
+    steps = 2
     width = DP * PAD
     lanes = np.arange(width, dtype=np.int32)
     places = np.concatenate([np.stack([lanes % PAD, lanes // PAD]), np.zeros((6, width), np.int32)])
@@ -262,17 +263,42 @@
 
 
 def backward_kernel(
-    core_ref, own_ref, other_ref, slope_ref, normed_ref, gain_ref, transposed_ref,
-    low_ref, keep_ref, send_ref, sums_ref, paired_ref, sem,
+    core_ref, own_ref, other_ref, slope_hbm, normed_hbm, gain_ref, transposed_ref,
+    low_ref, keep_ref, send_ref, sums_ref, paired_ref, slope_all, normed_all, sems,
 ):
     step = pl.program_id(0)
-    fetch = pltpu.make_async_copy(transposed_ref, paired_ref, sem)
+    rows = normed_all.shape[0] // STEPS
+    depth = paired_ref.shape[0]
+    share = depth // (2 * STEPS)
+    fetches = [
+        pltpu.make_async_copy(
+            transposed_ref.at[pl.ds(part * share, share), :],
+            paired_ref.at[pl.ds(part * share, share), :],
+            sems.at[2 * STEPS + part],
+        )
+        for part in range(2 * STEPS)
+    ]
+
+    def chunk(source, target, place, sem):
+        part = pl.ds(place * rows, rows)
+        return pltpu.make_async_copy(source.at[part, :], target.at[part, :], sems.at[sem])
 
     @pl.when(step == 0)
     def _():
-        fetch.start()
-
-    rows = slope_ref.shape[0]
+        for place in range(STEPS):
+            chunk(slope_hbm, slope_all, place, 2 * place).start()
+            chunk(normed_hbm, normed_all, place, 2 * place + 1).start()
+        for fetch in fetches:
+            fetch.start()
+
+    here = pl.ds(pl.multiple_of(step * rows, 16), rows)
+    for place in range(STEPS):
+
+        @pl.when(step == place)
+        def _():
+            chunk(slope_hbm, slope_all, place, 2 * place).wait()
+            chunk(normed_hbm, normed_all, place, 2 * place + 1).wait()
+
     first = core_ref[0] == 0
     columns = []
     for link in range(2):
@@ -281,16 +307,16 @@
         columns.append(jnp.where(first, own, other))
         columns.append(jnp.where(first, other, own))
     upstream = jnp.concatenate(columns, axis=1)
-    normed = normed_ref[...]
+    normed = normed_all[here, :]
     channels = normed.shape[1]
-    grad_act = upstream * slope_ref[:, :channels]
+    grad_act = upstream * slope_all[here, :channels]
     weighted = grad_act * normed
     gain = parameter(gain_ref[...], 1)
     grad_normed = grad_act * gain
     grad_mean = jnp.sum(grad_normed, axis=1, keepdims=True) * (1.0 / channels)
     cross_mean = jnp.sum(weighted * gain, axis=1, keepdims=True) * (1.0 / channels)
-    grad_pre = slope_ref[:, channels : channels + 1] * (grad_normed - grad_mean - normed * cross_mean)
-    low_ref[pl.ds(pl.multiple_of(step * rows, 16), rows), :] = grad_pre.astype(jnp.bfloat16)
+    grad_pre = slope_all[here, channels : channels + 1] * (grad_normed - grad_mean - normed * cross_mean)
+    low_ref[here, :] = grad_pre.astype(jnp.bfloat16)
     sums = jnp.concatenate(
         [
             jnp.sum(grad_pre, axis=0, keepdims=True),
@@ -311,49 +337,59 @@
 
     @pl.when(step == pl.num_programs(0) - 1)
     def _():
-        fetch.wait()
-        depth = paired_ref.shape[0]
+        for fetch in fetches:
+            fetch.wait()
         for target_ref, which in ((send_ref, 1 - core_ref[0]), (keep_ref, core_ref[0])):
             places = [pl.ds(pl.multiple_of((2 * link + which) * LANES, LANES), LANES) for link in range(2)]
             columns = jnp.concatenate([low_ref[:, place] for place in places], axis=1)
             product = jnp.dot(paired_ref[...], columns, preferred_element_type=jnp.float32)
             for link in range(2):
-                target_ref[link, :depth] = product[:, link * LANES : (link + 1) * LANES]
-                target_ref[link, depth:] = sums_ref[:, places[link]]
+                part = product[:, link * LANES : (link + 1) * LANES]
+                target_ref[link, :depth] = part.astype(target_ref.dtype)
+        for link in range(2):
+            kept = pl.ds(pl.multiple_of((2 * link + core_ref[0]) * LANES, LANES), LANES)
+            keep_ref[link, depth:] = sums_ref[:, kept]
+            sent = pl.ds(pl.multiple_of((2 * link + 1 - core_ref[0]) * LANES, LANES), LANES)
+            value = sums_ref[:, sent]
+            high = value.astype(jnp.bfloat16).astype(jnp.float32)
+            send_ref[link, depth:] = jnp.concatenate([high, value - high], axis=0).astype(
+                jnp.bfloat16
+            )
 
 
 def backward(core, own, other, slope, normed, gain, transposed):
-    steps = 4
     rows, channels = normed.shape
     depth = transposed.shape[0]
-    tile = rows // steps
-    frames = FRAMES // steps
+    frames = FRAMES // STEPS
     half = jax.ShapeDtypeStruct((2, depth + 8, LANES), jnp.float32)
+    leaving = jax.ShapeDtypeStruct((2, depth + 16, LANES), jnp.bfloat16)
     return pl.pallas_call(
         backward_kernel,
         grid_spec=pltpu.PrefetchScalarGridSpec(
             num_scalar_prefetch=1,
-            grid=(steps,),
+            grid=(STEPS,),
             in_specs=[
                 pl.BlockSpec((1, frames, 2, PAD, LANES), lambda i, core: (core[0], i, 0, 0, 0)),
                 pl.BlockSpec((frames, 2, PAD, LANES), lambda i, core: (i, 0, 0, 0)),
-                pl.BlockSpec((tile, channels + LANES), lambda i, core: (i, 0)),
-                pl.BlockSpec((tile, channels), lambda i, core: (i, 0)),
+                pl.BlockSpec(memory_space=pl.ANY),
+                pl.BlockSpec(memory_space=pl.ANY),
                 pl.BlockSpec((16, channels), lambda i, core: (depth // 16, 0)),
                 pl.BlockSpec(memory_space=pl.ANY),
             ],
             out_specs=(
                 pl.BlockSpec((rows, channels), lambda i, core: (0, 0)),
                 pl.BlockSpec(half.shape, lambda i, core: (0, 0, 0)),
-                pl.BlockSpec(half.shape, lambda i, core: (0, 0, 0)),
+                pl.BlockSpec(leaving.shape, lambda i, core: (0, 0, 0)),
             ),
             scratch_shapes=[
                 pltpu.VMEM((8, channels), jnp.float32),
                 pltpu.VMEM((depth, rows), jnp.bfloat16),
-                pltpu.SemaphoreType.DMA,
+                pltpu.VMEM((rows, channels + LANES), jnp.float32),
+                pltpu.VMEM((rows, channels), jnp.float32),
+                pltpu.SemaphoreType.DMA((4 * STEPS,)),
             ],
         ),
-        out_shape=(jax.ShapeDtypeStruct((rows, channels), jnp.bfloat16), half, half),
+        out_shape=(jax.ShapeDtypeStruct((rows, channels), jnp.bfloat16), half, leaving),
         compiler_params=pltpu.CompilerParams(vmem_limit_bytes=48 * MIB),
         cost_estimate=pl.CostEstimate(
             flops=2 * rows * depth * channels, bytes_accessed=9000000, transcendentals=0
@@ -399,10 +435,11 @@
 
 
 def chip_kernel(keep_ref, other_ref, weight_ref, vector_ref):
-    total = keep_ref[0] + other_ref[0]
-    depth = total.shape[0] - 8
-    weight_ref[:, 0] = total[:depth].reshape(DP, depth // DP, LANES).astype(jnp.bfloat16)
-    vector_ref[0] = total[depth:]
+    depth = keep_ref.shape[1] - 8
+    total = keep_ref[0, :depth] + other_ref[0, :depth].astype(jnp.float32)
+    weight_ref[:, 0] = total.reshape(DP, depth // DP, LANES).astype(jnp.bfloat16)
+    terms = other_ref[0, depth:].astype(jnp.float32)
+    vector_ref[0] = keep_ref[0, depth:] + (terms[:8] + terms[8:])
 
 
 def chip_total(keep, other):
@@ -414,7 +451,10 @@
             jax.ShapeDtypeStruct((DP, 2, depth // DP, LANES), jnp.bfloat16),
             jax.ShapeDtypeStruct((2, 8, LANES), jnp.float32),
         ),
-        in_specs=[pl.BlockSpec((1, depth + 8, LANES), lambda i: (i, 0, 0))] * 2,
+        in_specs=[
+            pl.BlockSpec((1, depth + 8, LANES), lambda i: (i, 0, 0)),
+            pl.BlockSpec((1, depth + 16, LANES), lambda i: (i, 0, 0)),
+        ],
         out_specs=(
             pl.BlockSpec((DP, 1, depth // DP, LANES), lambda i: (0, i, 0, 0)),
             pl.BlockSpec((1, 8, LANES), lambda i: (i, 0, 0)),

time: 139 us -> 138 us (level)
  Pallas kernels: 18.5 us -> 16.7 us
  local copies, waits for them, and re-layouts: 8.76 us -> 10.2 us
    all_to_all x1, waiting for transfers between devices: 16.9 us -> 15 us  [on_device(): lax.all_to_all(chip_weight.reshape(2 * DP, 16, LANES), ('dp', 'l'), split...]
    ppermute x7, waiting for transfers between devices: 6.09 us -> 7.83 us  [swap(): return lax.ppermute(value, axis, [(0, 1), (1, 0)])]
    unnamed x24 -> x26, local copies, waits for them, and re-layouts: 3.54 us -> 4.95 us
  transfers between devices with their start and end apart: 11 -> 11, of which waited for: 8 -> 9; matrix products, arithmetic and copies ran while one was open for 7% -> 7% of each run, Pallas kernels for 8% -> 7%
where the time goes in v1:
time: 138 us
  waiting for transfers between devices  66.4 us (48%)
  starting transfers between devices  37.6 us (27%)
  Pallas kernels  16.7 us (12%)
  local copies, waits for them, and re-layouts  10.2 us (7%)
  other arithmetic  5.9 us (4%)
    all_to_all x1, waiting for transfers between devices, route(): lax.all_to_all(outgoing, 'dp', split_axis=0, concat_axis=0, tiled=True)  18.9 us
    all_to_all x1, waiting for transfers between devices, on_device(): lax.all_to_all(chip_weight.reshape(2 * DP, 16, LANES), ('dp', 'l'), split...  15 us
    all_to_all x1, starting transfers between devices, route(): lax.all_to_all(outgoing, 'dp', split_axis=0, concat_axis=0, tiled=True)  13.7 us
    all_to_all x1, waiting for transfers between devices, route(): lax.all_to_all(sorted_pieces, ('dp', 'l'), split_axis=0, concat_axis=0, t...  13.1 us
    all_to_all x1, waiting for transfers between devices, on_device(): lax.all_to_all(jnp.broadcast_to(announce, (DP, PAD, LANES)), 'dp', split_...  11.6 us
    all_to_all x1, starting transfers between devices, route(): lax.all_to_all(sorted_pieces, ('dp', 'l'), split_axis=0, concat_axis=0, t...  7.87 us
    ppermute x7, waiting for transfers between devices, swap(): return lax.ppermute(value, axis, [(0, 1), (1, 0)])  7.83 us
    all_to_all x1, starting transfers between devices, on_device(): lax.all_to_all(chip_weight.reshape(2 * DP, 16, LANES), ('dp', 'l'), split...  6.92 us
  transfers between devices with their start and end apart: 11, of which 9 were waited for; matrix products, arithmetic and copies ran while one was open for 7% of the time, Pallas kernels for 7%

profile of v1, /device:TPU:2, one launch (start us, length us, event | category | flops | bytes accessed | tf_op | source)
XLA Modules:
  0.0 137.7 jit_solution(15909067444373922636)
XLA Ops:
  0.6 0.0 copy-start.1
  0.6 3.1 %shard_map.137 = bf16[64,2,24,128]{3,2,1,0:T(8,128)(2,1)} custom-call(bf16[2688,128]{1,0:T(8,128)(2,1)} %rows_ref.1, s32[21]{0:T(128)} %owner_ref.1, s32[21]{0:T(128)} %slot_ref.1), custom_call_target="tpu_custom_call" | custom-call | bytes 1500000 | tf_op jit(solution)/shard_map/pallas_call | solution.py:78
  3.7 13.7 %all-to-all-start = ((bf16[64,2,24,128]{3,2,1,0:T(8,128)(2,1)}), bf16[64,2,24,128]{3,2,1,0:T(8,128)(2,1)S(1)}, u32[]{:S(2)}, u32[]{:S(2)}) async-start(bf16[64,2,24,128]{3,2,1,0:T(8,128)(2,1)} %shard_map.137), calls=%async_computation | async-start | bytes 1572864 | tf_op jit(solution)/shard_map/all_to_all | solution.py:471
  17.4 0.0 copy-start.10
  17.4 0.0 copy-start.11
  17.4 0.0 copy-start.12
  17.5 0.0 copy-done.1
  17.5 0.1 copy.17
  17.6 0.0 copy-start.6
  17.6 0.0 copy-start.8
  17.6 0.4 copy-done.10
  18.1 0.0 copy-done.11
  18.1 0.0 copy-done.12
  18.1 0.1 constant_dynamic-slice_fusion.1
  18.2 0.5 copy-done.6
  18.7 0.1 copy-done.8
  18.8 1.0 pad_maximum_fusion.4
  19.8 1.4 %collective-permute-start = (bf16[3728,128]{1,0:T(8,128)(2,1)}, bf16[3728,128]{1,0:T(8,128)(2,1)S(1)}, u32[]{:S(2)}, u32[]{:S(2)}) collective-permute-start(bf16[3728,128]{1,0:T(8,128)(2,1)} %pad_maximum_fusion.4), channel_id=1, source_target_pairs={{0,2},{2,0},{1,3},{3,1},{4,6},{6,4},{5,7},{7,5},{8,10},{10,8},{9,1... | collective-permute-start | bytes 2863112 | tf_op jit(solution)/shard_map/ppermute | solution.py:37
  21.2 1.0 dynamic-slice_bitcast_fusion.1
  22.2 0.0 copy-done.9
  22.2 0.9 maximum_bitcast_fusion
  23.1 18.9 %all-to-all-done.spread_ref = bf16[64,2,24,128]{3,2,1,0:T(8,128)(2,1)S(1)} async-done(((bf16[64,2,24,128]{3,2,1,0:T(8,128)(2,1)}), bf16[64,2,24,128]{3,2,1,0:T(8,128)(2,1)S(1)}, u32[]{:S(2)}, u32[]{:S(2)}) %all-to-all-start) | async-done | bytes 786464 | tf_op jit(solution)/shard_map/all_to_all | solution.py:471
  42.0 2.8 %shard_map.138 = bf16[64,2,24,128]{3,2,1,0:T(8,128)(2,1)} custom-call(s32[8,1536]{1,0:T(8,128)S(1)} %copy-done.5, bf16[64,2,24,128]{3,2,1,0:T(8,128)(2,1)S(1)} %all-to-all-done.spread_ref), custom_call_target="tpu_custom_call" | custom-call | flops 4831838208 | bytes 1600000 | tf_op jit(solution)/shard_map/pallas_call | solution.py:133
  44.8 7.9 %all-to-all-start.1 = ((bf16[128,24,128]{2,1,0:T(8,128)(2,1)}), bf16[128,24,128]{2,1,0:T(8,128)(2,1)S(1)}, u32[]{:S(2)}, u32[]{:S(2)}) async-start(bf16[128,24,128]{2,1,0:T(8,128)(2,1)} %bitcast.1), calls=%async_computation.1 | async-start | bytes 1572864 | tf_op jit(solution)/shard_map/all_to_all | solution.py:473
  52.7 0.0 collective-permute-done.link_ref
  52.7 0.0 copy-start.2
  52.8 1.3 copy-done.7
  54.1 0.1 pad_maximum_fusion.3
  54.2 0.1 collective-permute-start.1
  54.3 0.1 pad_add_fusion.place_ref
  54.4 2.8 %collective-permute-done.1.beside_ref = bf16[2,2384,128]{2,1,0:T(8,128)(2,1)S(1)} collective-permute-done((bf16[2,2384,128]{2,1,0:T(8,128)(2,1)S(1)}, bf16[2,2384,128]{2,1,0:T(8,128)(2,1)S(1)}, u32[]{:S(2)}, u32[]{:S(2)}) %collective-permute-start.1) | collective-permute-done | bytes 1220640 | tf_op jit(solution)/shard_map/ppermute | solution.py:37
  57.2 1.2 copy-done.3
  58.4 5.7 %shard_map.139 = (bf16[1024,768]{1,0:T(8,128)(2,1)}, f32[768,640]{1,0:T(8,128)}, f32[768,512]{1,0:T(8,128)}, bf16[1040,512]{1,0:T(8,128)(2,1)S(1)}) custom-call(s32[2]{0:T(128)S(1)} %pad_add_fusion.place_ref, s32[3]{0:T(128)S(1)} %copy-done.4, bf16[21,4,64,128]{3,2,1,0:T(8,128)(2,1)S(1)} %bitcast.57, bf16[1040,128]{1,0:T(8,128)(2,1)S(1)} %pad_maximum_fusion.5.packed_ref, ...), custom_call_target="tpu_custom_call" | custom-call | flops 2415919104 | bytes 8000000 | tf_op jit(solution)/shard_map/pallas_call | solution.py:225
  64.0 13.1 %all-to-all-done.1 = bf16[128,24,128]{2,1,0:T(8,128)(2,1)S(1)} async-done(((bf16[128,24,128]{2,1,0:T(8,128)(2,1)}), bf16[128,24,128]{2,1,0:T(8,128)(2,1)S(1)}, u32[]{:S(2)}, u32[]{:S(2)}) %all-to-all-start.1) | async-done | bytes 786464 | tf_op jit(solution)/shard_map/all_to_all | solution.py:473
  77.1 0.1 collective-permute-start.2
  77.2 1.7 %collective-permute-done.2.other_ref = bf16[32,2,24,128]{3,2,1,0:T(8,128)(2,1)S(1)} collective-permute-done((bf16[32,2,24,128]{3,2,1,0:T(8,128)(2,1)S(1)}, bf16[32,2,24,128]{3,2,1,0:T(8,128)(2,1)S(1)}, u32[]{:S(2)}, u32[]{:S(2)}) %collective-permute-start.2) | collective-permute-done | bytes 393248 | tf_op jit(solution)/shard_map/ppermute | solution.py:37
  78.9 1.4 %copy-done = f32[768,512]{1,0:T(8,128)S(1)} copy-done((f32[768,512]{1,0:T(8,128)S(1)}, f32[768,512]{1,0:T(8,128)}, u32[]{:S(2)}) %copy-start) | copy-done | bytes 1572888
  80.4 3.3 %shard_map.140 = (bf16[768,512]{1,0:T(8,128)(2,1)S(1)}, f32[2,1032,128]{2,1,0:T(8,128)S(1)}, bf16[2,1040,128]{2,1,0:T(8,128)(2,1)S(1)}) custom-call(s32[1]{0:T(128)} %bitcast.core_ref, bf16[2,32,2,24,128]{4,3,2,1,0:T(8,128)(2,1)S(1)} %bitcast.53, bf16[32,2,24,128]{3,2,1,0:T(8,128)(2,1)S(1)} %collective-permute-done.2.other_ref, ...), custom_call_target="tpu_custom_call" | custom-call | flops 805306368 | bytes 9000000 | tf_op jit(solution)/shard_map/pallas_call | solution.py:366
  83.7 0.4 collective-permute-start.5
  84.1 1.0 shard_map.141
  85.1 0.5 collective-permute-start.3
  85.6 0.3 collective-permute-done.5.other_ref
  85.9 0.9 shard_map.142
  86.7 6.9 %all-to-all-start.2 = ((bf16[128,16,128]{2,1,0:T(8,128)(2,1)}), bf16[128,16,128]{2,1,0:T(8,128)(2,1)S(1)}, u32[]{:S(2)}, u32[]{:S(2)}) async-start(bf16[128,16,128]{2,1,0:T(8,128)(2,1)} %bitcast.26), calls=%async_computation.2 | async-start | bytes 1048576 | tf_op jit(solution)/shard_map/all_to_all | solution.py:527
  93.7 1.1 collective-permute-start.6
  94.8 0.1 pad.8.clone
  94.9 2.6 %collective-permute-done.6 = f32[8,128]{1,0:T(8,128)S(1)} collective-permute-done((f32[8,128]{1,0:T(8,128)S(1)}, f32[8,128]{1,0:T(8,128)S(1)}, u32[]{:S(2)}, u32[]{:S(2)}) %collective-permute-start.6) | collective-permute-done | bytes 4128 | tf_op jit(solution)/shard_map/ppermute | solution.py:37
  97.5 0.0 collective-permute-done.3
  97.5 1.0 fusion.2
  98.4 0.9 collective-permute-start.4
  99.3 15.0 %all-to-all-done.2 = bf16[128,16,128]{2,1,0:T(8,128)(2,1)S(1)} async-done(((bf16[128,16,128]{2,1,0:T(8,128)(2,1)}), bf16[128,16,128]{2,1,0:T(8,128)(2,1)S(1)}, u32[]{:S(2)}, u32[]{:S(2)}) %all-to-all-start.2) | async-done | bytes 524320 | tf_op jit(solution)/shard_map/all_to_all | solution.py:527
  114.4 0.1 convert_reduce_fusion
  114.5 0.1 maximum_maximum_fusion
  114.6 0.8 broadcast_in_dim.7
  115.4 4.6 %all-to-all-start.3 = ((bf16[64,24,128]{2,1,0:T(8,128)(2,1)}), bf16[64,24,128]{2,1,0:T(8,128)(2,1)S(1)}, u32[]{:S(2)}, u32[]{:S(2)}) async-start(bf16[64,24,128]{2,1,0:T(8,128)(2,1)} %broadcast_in_dim.7), calls=%async_computation.3 | async-start | bytes 786432 | tf_op jit(solution)/shard_map/all_to_all | solution.py:535
  120.1 0.4 collective-permute-done.4
  120.4 1.2 broadcast_select_fusion.1
  121.7 0.1 broadcast_select_fusion.3
  121.8 0.3 fusion
  122.1 2.5 %copy.18 = bf16[21,4,32,2,128]{4,3,2,1,0:T(2,128)(2,1)} copy(bf16[21,4,32,2,128]{4,0,2,3,1:T(8,128)(2,1)S(1)} %fusion) | data formatting | bytes 2752512 | tf_op jit(solution)/shard_map/transpose | solution.py:553
  124.6 11.6 %all-to-all-done.3 = bf16[64,24,128]{2,1,0:T(8,128)(2,1)S(1)} async-done(((bf16[64,24,128]{2,1,0:T(8,128)(2,1)}), bf16[64,24,128]{2,1,0:T(8,128)(2,1)S(1)}, u32[]{:S(2)}, u32[]{:S(2)}) %all-to-all-start.3) | async-done | bytes 393248 | tf_op jit(solution)/shard_map/all_to_all | solution.py:535
  136.2 0.8 bitcast_convert_fusion
  137.1 0.1 convert_reduce_fusion.1
  137.2 0.5 slice_bitcast_fusion
  (23 shorter events, 0.3 us)
Async XLA Ops:
  0.6 16.8 %copy-start.1 = (bf16[5376,128]{1,0:T(8,128)(2,1)S(1)}, bf16[5376,128]{1,0:T(8,128)(2,1)}, u32[]{:S(2)}) copy-start(bf16[5376,128]{1,0:T(8,128)(2,1)} %param.10) | copy-start | bytes 4128772
  3.7 38.2 %all-to-all-start = ((bf16[64,2,24,128]{3,2,1,0:T(8,128)(2,1)}), bf16[64,2,24,128]{3,2,1,0:T(8,128)(2,1)S(1)}, u32[]{:S(2)}, u32[]{:S(2)}) async-start(bf16[64,2,24,128]{3,2,1,0:T(8,128)(2,1)} %shard_map.137), calls=%async_computation | async-start | bytes 1572864 | tf_op jit(solution)/shard_map/all_to_all | solution.py:471
  17.4 0.7 copy-start.10
  17.4 0.7 copy-start.11
  17.4 0.7 copy-start.12
  17.6 1.1 copy-start.6
  17.6 1.1 copy-start.8
  18.8 3.5 %copy-start.9 = (bf16[1024,128]{1,0:T(8,128)(2,1)S(1)}, bf16[1024,128]{1,0:T(8,128)(2,1)}, u32[]{:S(2)}) copy-start(bf16[1024,128]{1,0:T(8,128)(2,1)} %param.11) | copy-start | bytes 786436
  18.8 23.2 %copy-start.5 = (s32[8,1536]{1,0:T(8,128)S(1)}, s32[8,1536]{1,0:T(8,128)}, u32[]{:S(2)}) copy-start(s32[8,1536]{1,0:T(8,128)} %constant.74.clone.lane_ref) | copy-start | bytes 147460
  19.8 32.9 %collective-permute-start = (bf16[3728,128]{1,0:T(8,128)(2,1)}, bf16[3728,128]{1,0:T(8,128)(2,1)S(1)}, u32[]{:S(2)}, u32[]{:S(2)}) collective-permute-start(bf16[3728,128]{1,0:T(8,128)(2,1)} %pad_maximum_fusion.4), channel_id=1, source_target_pairs={{0,2},{2,0},{1,3},{3,1},{4,6},{6,4},{5,7},{7,5},{8,10},{10,8},{9,1... | collective-permute-start | bytes 2863112 | tf_op jit(solution)/shard_map/ppermute | solution.py:37
  44.8 32.3 %all-to-all-start.1 = ((bf16[128,24,128]{2,1,0:T(8,128)(2,1)}), bf16[128,24,128]{2,1,0:T(8,128)(2,1)S(1)}, u32[]{:S(2)}, u32[]{:S(2)}) async-start(bf16[128,24,128]{2,1,0:T(8,128)(2,1)} %bitcast.1), calls=%async_computation.1 | async-start | bytes 1572864 | tf_op jit(solution)/shard_map/all_to_all | solution.py:473
  52.6 1.4 %copy-start.7 = (bf16[1,2384,128]{2,1,0:T(8,128)(2,1)S(1)}, bf16[1,2384,128]{2,1,0:T(8,128)(2,1)}, u32[]{:S(2)}) copy-start(bf16[1,2384,128]{2,1,0:T(8,128)(2,1)} %maximum_bitcast_fusion) | copy-start | bytes 1830916
  52.7 1.5 %copy-start.2 = (bf16[3728,128]{1,0:T(8,128)(2,1)}, bf16[3728,128]{1,0:T(8,128)(2,1)S(1)}, u32[]{:S(2)}) copy-start(bf16[3728,128]{1,0:T(8,128)(2,1)S(1)} %collective-permute-done.link_ref) | copy-start | bytes 2863108
  54.1 3.1 %copy-start.4 = (s32[3]{0:T(128)S(1)}, s32[3]{0:T(128)}, u32[]{:S(2)}) copy-start(s32[3]{0:T(128)} %lengths_ref.1) | copy-start | bytes 40
  54.2 3.0 %collective-permute-start.1 = (bf16[2,2384,128]{2,1,0:T(8,128)(2,1)S(1)}, bf16[2,2384,128]{2,1,0:T(8,128)(2,1)S(1)}, u32[]{:S(2)}, u32[]{:S(2)}) collective-permute-start(bf16[2,2384,128]{2,1,0:T(8,128)(2,1)S(1)} %pad_maximum_fusion.3), channel_id=1, source_target_pairs={{0,1},{1,0},{2,3},{3,2},{4,5},{5,4},{6,7},{7,6},{8,9},{9,8},{10,11... | collective-permute-start | bytes 3661832 | tf_op jit(solution)/shard_map/ppermute | solution.py:37
  57.2 1.2 copy-start.3
  77.1 1.8 %collective-permute-start.2 = (bf16[32,2,24,128]{3,2,1,0:T(8,128)(2,1)S(1)}, bf16[32,2,24,128]{3,2,1,0:T(8,128)(2,1)S(1)}, u32[]{:S(2)}, u32[]{:S(2)}) collective-permute-start(bf16[32,2,24,128]{3,2,1,0:T(8,128)(2,1)S(1)} %dynamic-slice_bitcast_fusion), channel_id=1, source_target_pairs={{0,1},{1,0},{2,3},{3,2},{4,5},{5,4},{6,7},{7,6},{8,9},{9,8},{10,11... | collective-permute-start | bytes 1179656 | tf_op jit(solution)/shard_map/ppermute | solution.py:37
  78.9 1.4 %copy-start = (f32[768,512]{1,0:T(8,128)S(1)}, f32[768,512]{1,0:T(8,128)}, u32[]{:S(2)}) copy-start(f32[768,512]{1,0:T(8,128)} %get-tuple-element.19.normed_hbm) | copy-start | bytes 4718596
  83.7 2.2 %collective-permute-start.5 = (bf16[2,1040,128]{2,1,0:T(8,128)(2,1)S(1)}, bf16[2,1040,128]{2,1,0:T(8,128)(2,1)S(1)}, u32[]{:S(2)}, u32[]{:S(2)}) collective-permute-start(bf16[2,1040,128]{2,1,0:T(8,128)(2,1)S(1)} %get-tuple-element.28), channel_id=1, source_target_pairs={{0,1},{1,0},{2,3},{3,2},{4,5},{5,4},{6,7},{7,6},{8,9},{9,8},{10,11... | collective-permute-start | bytes 1597448 | tf_op jit(solution)/shard_map/ppermute | solution.py:37
  85.1 12.4 %collective-permute-start.3 = (bf16[2,2,768,128]{3,2,1,0:T(8,128)(2,1)S(1)}, bf16[2,2,768,128]{3,2,1,0:T(8,128)(2,1)S(1)}, u32[]{:S(2)}, u32[]{:S(2)}) collective-permute-start(bf16[2,2,768,128]{3,2,1,0:T(8,128)(2,1)S(1)} %get-tuple-element.26), channel_id=1, source_target_pairs={{0,1},{1,0},{2,3},{3,2},{4,5},{5,4},{6,7},{7,6},{8,9},{9,8},{10,11... | collective-permute-start | bytes 2359304 | tf_op jit(solution)/shard_map/ppermute | solution.py:37
  86.7 27.6 %all-to-all-start.2 = ((bf16[128,16,128]{2,1,0:T(8,128)(2,1)}), bf16[128,16,128]{2,1,0:T(8,128)(2,1)S(1)}, u32[]{:S(2)}, u32[]{:S(2)}) async-start(bf16[128,16,128]{2,1,0:T(8,128)(2,1)} %bitcast.26), calls=%async_computation.2 | async-start | bytes 1048576 | tf_op jit(solution)/shard_map/all_to_all | solution.py:527
  93.7 3.8 %collective-permute-start.6 = (f32[8,128]{1,0:T(8,128)S(1)}, f32[8,128]{1,0:T(8,128)S(1)}, u32[]{:S(2)}, u32[]{:S(2)}) collective-permute-start(f32[8,128]{1,0:T(8,128)S(1)} %dynamic-slice_bitcast_fusion.2), channel_id=1, source_target_pairs={{0,2},{2,0},{1,3},{3,1},{4,6},{6,4},{5,7},{7,5},{8,10},{10,8},{9,1... | collective-permute-start | bytes 12296 | tf_op jit(solution)/shard_map/ppermute | solution.py:37
  98.4 22.0 %collective-permute-start.4 = (bf16[2,2,768,128]{3,2,1,0:T(8,128)(2,1)}, bf16[2,2,768,128]{3,2,1,0:T(8,128)(2,1)}, u32[]{:S(2)}, u32[]{:S(2)}) collective-permute-start(bf16[2,2,768,128]{3,2,1,0:T(8,128)(2,1)} %fusion.2), channel_id=1, source_target_pairs={{0,2},{2,0},{1,3},{3,1},{4,6},{6,4},{5,7},{7,5},{8,10},{10,8},{9,1... | collective-permute-start | bytes 2359304 | tf_op jit(solution)/shard_map/ppermute | solution.py:37
  115.4 20.8 %all-to-all-start.3 = ((bf16[64,24,128]{2,1,0:T(8,128)(2,1)}), bf16[64,24,128]{2,1,0:T(8,128)(2,1)S(1)}, u32[]{:S(2)}, u32[]{:S(2)}) async-start(bf16[64,24,128]{2,1,0:T(8,128)(2,1)} %broadcast_in_dim.7), calls=%async_computation.3 | async-start | bytes 786432 | tf_op jit(solution)/shard_map/all_to_all | solution.py:535

commit v2 on v1

--- a/solution.py
+++ b/solution.py
@@ -14,11 +14,12 @@
 PAD = 24
 DP = 64
 LANES = 128
-STEPS = 2
+STEPS = 4
 FRAMES = 32
 
 MIB = 1024 * 1024
 VMEM = 28 * MIB
+BRING = 52 * MIB
 ALL_VMEM = 60 * MIB
 
 EPSILON = 1e-05
@@ -262,43 +263,43 @@
     )(jnp.stack([link, core]), lengths, feats, packed, from_link, from_core)
 
 
+def bring_kernel(slope_hbm, normed_hbm, transposed_hbm, slope_ref, normed_ref, transposed_ref, sems):
+    copies = []
+    for source, target in (
+        (slope_hbm, slope_ref), (normed_hbm, normed_ref), (transposed_hbm, transposed_ref)
+    ):
+        share = source.shape[0] // 4
+        for part in range(4):
+            place = pl.ds(part * share, share)
+            copies.append(
+                pltpu.make_async_copy(source.at[place, :], target.at[place, :], sems.at[len(copies)])
+            )
+    for copy in copies:
+        copy.start()
+    for copy in copies:
+        copy.wait()
+
+
+def bring(slope, normed, transposed):
+    arrays = (slope, normed, transposed)
+    return pl.pallas_call(
+        bring_kernel,
+        out_shape=tuple(pltpu.VMEM(array.shape, array.dtype) for array in arrays),
+        in_specs=[pl.BlockSpec(memory_space=pl.ANY)] * 3,
+        out_specs=(pl.BlockSpec(memory_space=pltpu.VMEM),) * 3,
+        scratch_shapes=[pltpu.SemaphoreType.DMA((12,))],
+        compiler_params=pltpu.CompilerParams(vmem_limit_bytes=BRING),
+        cost_estimate=pl.CostEstimate(flops=0, bytes_accessed=10000000, transcendentals=0),
+    )(*arrays)
+
+
 def backward_kernel(
-    core_ref, own_ref, other_ref, slope_hbm, normed_hbm, gain_ref, transposed_ref,
-    low_ref, keep_ref, send_ref, sums_ref, paired_ref, slope_all, normed_all, sems,
+    core_ref, own_ref, other_ref, slope_ref, normed_ref, gain_ref, transposed_ref,
+    low_ref, keep_ref, send_ref, sums_ref,
 ):
     step = pl.program_id(0)
-    rows = normed_all.shape[0] // STEPS
-    depth = paired_ref.shape[0]
-    share = depth // (2 * STEPS)
-    fetches = [
-        pltpu.make_async_copy(
-            transposed_ref.at[pl.ds(part * share, share), :],
-            paired_ref.at[pl.ds(part * share, share), :],
-            sems.at[2 * STEPS + part],
-        )
-        for part in range(2 * STEPS)
-    ]
-
-    def chunk(source, target, place, sem):
-        part = pl.ds(place * rows, rows)
-        return pltpu.make_async_copy(source.at[part, :], target.at[part, :], sems.at[sem])
-
-    @pl.when(step == 0)
-    def _():
-        for place in range(STEPS):
-            chunk(slope_hbm, slope_all, place, 2 * place).start()
-            chunk(normed_hbm, normed_all, place, 2 * place + 1).start()
-        for fetch in fetches:
-            fetch.start()
-
+    rows = normed_ref.shape[0]
     here = pl.ds(pl.multiple_of(step * rows, 16), rows)
-    for place in range(STEPS):
-
-        @pl.when(step == place)
-        def _():
-            chunk(slope_hbm, slope_all, place, 2 * place).wait()
-            chunk(normed_hbm, normed_all, place, 2 * place + 1).wait()
-
     first = core_ref[0] == 0
     columns = []
     for link in range(2):
@@ -307,15 +308,15 @@
         columns.append(jnp.where(first, own, other))
         columns.append(jnp.where(first, other, own))
     upstream = jnp.concatenate(columns, axis=1)
-    normed = normed_all[here, :]
+    normed = normed_ref[...]
     channels = normed.shape[1]
-    grad_act = upstream * slope_all[here, :channels]
+    grad_act = upstream * slope_ref[:, :channels]
     weighted = grad_act * normed
     gain = parameter(gain_ref[...], 1)
     grad_normed = grad_act * gain
     grad_mean = jnp.sum(grad_normed, axis=1, keepdims=True) * (1.0 / channels)
     cross_mean = jnp.sum(weighted * gain, axis=1, keepdims=True) * (1.0 / channels)
-    grad_pre = slope_all[here, channels : channels + 1] * (grad_normed - grad_mean - normed * cross_mean)
+    grad_pre = slope_ref[:, channels : channels + 1] * (grad_normed - grad_mean - normed * cross_mean)
     low_ref[here, :] = grad_pre.astype(jnp.bfloat16)
     sums = jnp.concatenate(
         [
@@ -337,12 +338,11 @@
 
     @pl.when(step == pl.num_programs(0) - 1)
     def _():
-        for fetch in fetches:
-            fetch.wait()
+        depth = transposed_ref.shape[0]
         for target_ref, which in ((send_ref, 1 - core_ref[0]), (keep_ref, core_ref[0])):
             places = [pl.ds(pl.multiple_of((2 * link + which) * LANES, LANES), LANES) for link in range(2)]
             columns = jnp.concatenate([low_ref[:, place] for place in places], axis=1)
-            product = jnp.dot(paired_ref[...], columns, preferred_element_type=jnp.float32)
+            product = jnp.dot(transposed_ref[...], columns, preferred_element_type=jnp.float32)
             for link in range(2):
                 part = product[:, link * LANES : (link + 1) * LANES]
                 target_ref[link, :depth] = part.astype(target_ref.dtype)
@@ -371,26 +371,20 @@
             in_specs=[
                 pl.BlockSpec((1, frames, 2, PAD, LANES), lambda i, core: (core[0], i, 0, 0, 0)),
                 pl.BlockSpec((frames, 2, PAD, LANES), lambda i, core: (i, 0, 0, 0)),
-                pl.BlockSpec(memory_space=pl.ANY),
-                pl.BlockSpec(memory_space=pl.ANY),
+                pl.BlockSpec((rows // STEPS, channels + LANES), lambda i, core: (i, 0)),
+                pl.BlockSpec((rows // STEPS, channels), lambda i, core: (i, 0)),
                 pl.BlockSpec((16, channels), lambda i, core: (depth // 16, 0)),
-                pl.BlockSpec(memory_space=pl.ANY),
+                pl.BlockSpec((depth, rows), lambda i, core: (0, 0)),
             ],
             out_specs=(
                 pl.BlockSpec((rows, channels), lambda i, core: (0, 0)),
                 pl.BlockSpec(half.shape, lambda i, core: (0, 0, 0)),
                 pl.BlockSpec(leaving.shape, lambda i, core: (0, 0, 0)),
             ),
-            scratch_shapes=[
-                pltpu.VMEM((8, channels), jnp.float32),
-                pltpu.VMEM((depth, rows), jnp.bfloat16),
-                pltpu.VMEM((rows, channels + LANES), jnp.float32),
-                pltpu.VMEM((rows, channels), jnp.float32),
-                pltpu.SemaphoreType.DMA((4 * STEPS,)),
-            ],
+            scratch_shapes=[pltpu.VMEM((8, channels), jnp.float32)],
         ),
         out_shape=(jax.ShapeDtypeStruct((rows, channels), jnp.bfloat16), half, leaving),
-        compiler_params=pltpu.CompilerParams(vmem_limit_bytes=48 * MIB),
+        compiler_params=pltpu.CompilerParams(vmem_limit_bytes=28 * MIB),
         cost_estimate=pl.CostEstimate(
             flops=2 * rows * depth * channels, bytes_accessed=9000000, transcendentals=0
         ),
@@ -514,8 +508,11 @@
         link, core, lengths, feats.reshape(SLOTS, 4, 2 * FRAMES, LANES), packed, from_link, from_core
     )
 
-    leaving, _ = lax.optimization_barrier((pick(own, 1 - core, 0), normed))
+    leaving, slope, normed, transposed = lax.optimization_barrier(
+        (pick(own, 1 - core, 0), slope, normed, transposed)
+    )
     other = swap(leaving, "c")
+    slope, normed, transposed = bring(slope, normed, transposed)
 
     low, keep, send = backward(
         core, own, other, slope, normed, weight, transposed

time: 138 us -> 137 us (level)
  local copies, waits for them, and re-layouts: 10.2 us -> 8.77 us
  Pallas kernels: 16.7 us -> 18.1 us
    pallas_call x0 -> x1, Pallas kernels: none -> 2.52 us  [bring(): pl.pallas_call(bring_kernel, out_shape=tuple((pltpu.VMEM(array.shape, arr...]
    ppermute x7, waiting for transfers between devices: 7.83 us -> 5.77 us  [swap(): return lax.ppermute(value, axis, [(0, 1), (1, 0)])]
    unnamed x26 -> x24, local copies, waits for them, and re-layouts: 4.95 us -> 3.54 us
  transfers between devices with their start and end apart: 11 -> 11, of which waited for: 9 -> 7; matrix products, arithmetic and copies ran while one was open for 7% -> 6% of each run, Pallas kernels for 7% -> 9%
where the time goes in v2:
time: 137 us; the launch traced here: 136 us
  waiting for transfers between devices  65.6 us (48%)
  starting transfers between devices  37.8 us (28%)
  Pallas kernels  18.1 us (13%)
  local copies, waits for them, and re-layouts  8.77 us (6%)
  other arithmetic  5.07 us (4%)
    all_to_all x1, waiting for transfers between devices, route(): lax.all_to_all(outgoing, 'dp', split_axis=0, concat_axis=0, tiled=True)  18.9 us
    all_to_all x1, waiting for transfers between devices, on_device(): lax.all_to_all(chip_weight.reshape(2 * DP, 16, LANES), ('dp', 'l'), split...  16 us
    all_to_all x1, starting transfers between devices, route(): lax.all_to_all(outgoing, 'dp', split_axis=0, concat_axis=0, tiled=True)  13.7 us
    all_to_all x1, waiting for transfers between devices, route(): lax.all_to_all(sorted_pieces, ('dp', 'l'), split_axis=0, concat_axis=0, t...  13.1 us
    all_to_all x1, waiting for transfers between devices, on_device(): lax.all_to_all(jnp.broadcast_to(announce, (DP, PAD, LANES)), 'dp', split_...  12 us
    all_to_all x1, starting transfers between devices, route(): lax.all_to_all(sorted_pieces, ('dp', 'l'), split_axis=0, concat_axis=0, t...  7.87 us
    all_to_all x1, starting transfers between devices, on_device(): lax.all_to_all(chip_weight.reshape(2 * DP, 16, LANES), ('dp', 'l'), split...  6.93 us
    ppermute x7, waiting for transfers between devices, swap(): return lax.ppermute(value, axis, [(0, 1), (1, 0)])  5.77 us
  transfers between devices with their start and end apart: 11, of which 7 were waited for; matrix products, arithmetic and copies ran while one was open for 6% of the time, Pallas kernels for 9%

profile of v2, /device:TPU:2, one launch (start us, length us, event | category | flops | bytes accessed | tf_op | source)
XLA Modules:
  0.0 136.3 jit_solution(14589981834886821644)
XLA Ops:
  0.6 0.0 copy-start
  0.6 3.1 %shard_map.137 = bf16[64,2,24,128]{3,2,1,0:T(8,128)(2,1)} custom-call(bf16[2688,128]{1,0:T(8,128)(2,1)} %rows_ref.1, s32[21]{0:T(128)} %owner_ref.1, s32[21]{0:T(128)} %slot_ref.1), custom_call_target="tpu_custom_call" | custom-call | bytes 1500000 | tf_op jit(solution)/shard_map/pallas_call | solution.py:79
  3.7 13.7 %all-to-all-start = ((bf16[64,2,24,128]{3,2,1,0:T(8,128)(2,1)}), bf16[64,2,24,128]{3,2,1,0:T(8,128)(2,1)S(1)}, u32[]{:S(2)}, u32[]{:S(2)}) async-start(bf16[64,2,24,128]{3,2,1,0:T(8,128)(2,1)} %shard_map.137), calls=%async_computation | async-start | bytes 1572864 | tf_op jit(solution)/shard_map/all_to_all | solution.py:465
  17.4 0.0 copy-start.9
  17.4 0.0 copy-start.10
  17.4 0.0 copy-start.11
  17.5 0.0 copy-done
  17.5 0.1 copy.17
  17.6 0.0 copy-start.5
  17.6 0.0 copy-start.7
  17.6 0.4 copy-done.9
  18.1 0.0 copy-done.10
  18.1 0.0 copy-done.11
  18.1 0.1 constant_dynamic-slice_fusion.1
  18.2 0.5 copy-done.5
  18.7 0.1 copy-done.7
  18.8 1.0 pad_maximum_fusion.4
  19.8 1.4 %collective-permute-start = (bf16[3728,128]{1,0:T(8,128)(2,1)}, bf16[3728,128]{1,0:T(8,128)(2,1)S(1)}, u32[]{:S(2)}, u32[]{:S(2)}) collective-permute-start(bf16[3728,128]{1,0:T(8,128)(2,1)} %pad_maximum_fusion.4), channel_id=1, source_target_pairs={{0,2},{2,0},{1,3},{3,1},{4,6},{6,4},{5,7},{7,5},{8,10},{10,8},{9,1... | collective-permute-start | bytes 2863112 | tf_op jit(solution)/shard_map/ppermute | solution.py:38
  21.2 1.0 dynamic-slice_bitcast_fusion.1
  22.2 0.0 copy-done.8
  22.2 0.9 maximum_bitcast_fusion
  23.1 18.9 %all-to-all-done.spread_ref = bf16[64,2,24,128]{3,2,1,0:T(8,128)(2,1)S(1)} async-done(((bf16[64,2,24,128]{3,2,1,0:T(8,128)(2,1)}), bf16[64,2,24,128]{3,2,1,0:T(8,128)(2,1)S(1)}, u32[]{:S(2)}, u32[]{:S(2)}) %all-to-all-start) | async-done | bytes 786464 | tf_op jit(solution)/shard_map/all_to_all | solution.py:465
  42.0 2.8 %shard_map.138 = bf16[64,2,24,128]{3,2,1,0:T(8,128)(2,1)} custom-call(s32[8,1536]{1,0:T(8,128)S(1)} %copy-done.4, bf16[64,2,24,128]{3,2,1,0:T(8,128)(2,1)S(1)} %all-to-all-done.spread_ref), custom_call_target="tpu_custom_call" | custom-call | flops 4831838208 | bytes 1600000 | tf_op jit(solution)/shard_map/pallas_call | solution.py:134
  44.8 7.9 %all-to-all-start.1 = ((bf16[128,24,128]{2,1,0:T(8,128)(2,1)}), bf16[128,24,128]{2,1,0:T(8,128)(2,1)S(1)}, u32[]{:S(2)}, u32[]{:S(2)}) async-start(bf16[128,24,128]{2,1,0:T(8,128)(2,1)} %bitcast.1), calls=%async_computation.1 | async-start | bytes 1572864 | tf_op jit(solution)/shard_map/all_to_all | solution.py:467
  52.7 0.0 collective-permute-done.link_ref
  52.7 0.0 copy-start.1
  52.8 1.3 copy-done.6
  54.1 0.1 pad_maximum_fusion.3
  54.2 0.1 collective-permute-start.1
  54.3 0.1 pad_add_fusion.place_ref
  54.4 2.8 %collective-permute-done.1.beside_ref = bf16[2,2384,128]{2,1,0:T(8,128)(2,1)S(1)} collective-permute-done((bf16[2,2384,128]{2,1,0:T(8,128)(2,1)S(1)}, bf16[2,2384,128]{2,1,0:T(8,128)(2,1)S(1)}, u32[]{:S(2)}, u32[]{:S(2)}) %collective-permute-start.1) | collective-permute-done | bytes 1220640 | tf_op jit(solution)/shard_map/ppermute | solution.py:38
  57.2 1.2 copy-done.2
  58.4 5.7 %shard_map.139 = (bf16[1024,768]{1,0:T(8,128)(2,1)}, f32[768,640]{1,0:T(8,128)}, f32[768,512]{1,0:T(8,128)}, bf16[1040,512]{1,0:T(8,128)(2,1)S(1)}) custom-call(s32[2]{0:T(128)S(1)} %pad_add_fusion.place_ref, s32[3]{0:T(128)S(1)} %copy-done.3, bf16[21,4,64,128]{3,2,1,0:T(8,128)(2,1)S(1)} %bitcast.57, bf16[1040,128]{1,0:T(8,128)(2,1)S(1)} %pad_maximum_fusion.5.packed_ref, ...), custom_call_target="tpu_custom_call" | custom-call | flops 2415919104 | bytes 8000000 | tf_op jit(solution)/shard_map/pallas_call | solution.py:226
  64.0 13.1 %all-to-all-done.1 = bf16[128,24,128]{2,1,0:T(8,128)(2,1)S(1)} async-done(((bf16[128,24,128]{2,1,0:T(8,128)(2,1)}), bf16[128,24,128]{2,1,0:T(8,128)(2,1)S(1)}, u32[]{:S(2)}, u32[]{:S(2)}) %all-to-all-start.1) | async-done | bytes 786464 | tf_op jit(solution)/shard_map/all_to_all | solution.py:467
  77.1 0.1 collective-permute-start.2
  77.2 2.5 %shard_map.140 = (f32[768,640]{1,0:T(8,128)S(1)}, f32[768,512]{1,0:T(8,128)S(1)}, bf16[1024,768]{1,0:T(8,128)(2,1)S(1)}) custom-call(f32[768,640]{1,0:T(8,128)} %get-tuple-element.29.slope_hbm, f32[768,512]{1,0:T(8,128)} %get-tuple-element.30.normed_hbm, bf16[1024,768]{1,0:T(8,128)(2,1)} %get-tuple-element.31.transposed_hbm), custom_call_target="tpu_custom_call" | custom-call | bytes 10000000 | tf_op jit(solution)/shard_map/pallas_call | solution.py:285
  79.8 0.0 collective-permute-done.2.other_ref
  79.8 2.2 %shard_map.141 = (bf16[768,512]{1,0:T(8,128)(2,1)S(1)}, f32[2,1032,128]{2,1,0:T(8,128)S(1)}, bf16[2,1040,128]{2,1,0:T(8,128)(2,1)S(1)}) custom-call(s32[1]{0:T(128)} %bitcast.core_ref, bf16[2,32,2,24,128]{4,3,2,1,0:T(8,128)(2,1)S(1)} %bitcast.53, bf16[32,2,24,128]{3,2,1,0:T(8,128)(2,1)S(1)} %collective-permute-done.2.other_ref, ...), custom_call_target="tpu_custom_call" | custom-call | flops 805306368 | bytes 9000000 | tf_op jit(solution)/shard_map/pallas_call | solution.py:366
  82.0 0.8 collective-permute-start.5
  82.8 1.0 shard_map.142
  83.8 0.1 collective-permute-start.3
  83.9 0.4 collective-permute-done.5.other_ref
  84.3 0.9 shard_map.143
  85.2 6.9 %all-to-all-start.2 = ((bf16[128,16,128]{2,1,0:T(8,128)(2,1)}), bf16[128,16,128]{2,1,0:T(8,128)(2,1)S(1)}, u32[]{:S(2)}, u32[]{:S(2)}) async-start(bf16[128,16,128]{2,1,0:T(8,128)(2,1)} %bitcast.26), calls=%async_computation.2 | async-start | bytes 1048576 | tf_op jit(solution)/shard_map/all_to_all | solution.py:524
  92.1 1.1 collective-permute-start.6
  93.2 0.1 pad.8.clone
  93.3 2.5 %collective-permute-done.6 = f32[8,128]{1,0:T(8,128)S(1)} collective-permute-done((f32[8,128]{1,0:T(8,128)S(1)}, f32[8,128]{1,0:T(8,128)S(1)}, u32[]{:S(2)}, u32[]{:S(2)}) %collective-permute-start.6) | collective-permute-done | bytes 4128 | tf_op jit(solution)/shard_map/ppermute | solution.py:38
  95.8 0.0 collective-permute-done.3
  95.8 0.1 fusion.2
  95.9 1.1 collective-permute-start.4
  97.0 16.0 %all-to-all-done.2 = bf16[128,16,128]{2,1,0:T(8,128)(2,1)S(1)} async-done(((bf16[128,16,128]{2,1,0:T(8,128)(2,1)}), bf16[128,16,128]{2,1,0:T(8,128)(2,1)S(1)}, u32[]{:S(2)}, u32[]{:S(2)}) %all-to-all-start.2) | async-done | bytes 524320 | tf_op jit(solution)/shard_map/all_to_all | solution.py:524
  113.0 0.1 convert_reduce_fusion
  113.2 0.1 maximum_maximum_fusion
  113.2 0.8 broadcast_in_dim.7
  114.0 4.6 %all-to-all-start.3 = ((bf16[64,24,128]{2,1,0:T(8,128)(2,1)}), bf16[64,24,128]{2,1,0:T(8,128)(2,1)S(1)}, u32[]{:S(2)}, u32[]{:S(2)}) async-start(bf16[64,24,128]{2,1,0:T(8,128)(2,1)} %broadcast_in_dim.7), calls=%async_computation.3 | async-start | bytes 786432 | tf_op jit(solution)/shard_map/all_to_all | solution.py:532
  118.7 0.0 collective-permute-done.4
  118.7 1.2 broadcast_select_fusion.1
  119.9 0.2 broadcast_select_fusion.3
  120.1 0.3 fusion
  120.4 2.5 %copy.18 = bf16[21,4,32,2,128]{4,3,2,1,0:T(2,128)(2,1)} copy(bf16[21,4,32,2,128]{4,0,2,3,1:T(8,128)(2,1)S(1)} %fusion) | data formatting | bytes 2752512 | tf_op jit(solution)/shard_map/transpose | solution.py:550
  122.9 12.0 %all-to-all-done.3 = bf16[64,24,128]{2,1,0:T(8,128)(2,1)S(1)} async-done(((bf16[64,24,128]{2,1,0:T(8,128)(2,1)}), bf16[64,24,128]{2,1,0:T(8,128)(2,1)S(1)}, u32[]{:S(2)}, u32[]{:S(2)}) %all-to-all-start.3) | async-done | bytes 393248 | tf_op jit(solution)/shard_map/all_to_all | solution.py:532
  134.9 0.8 bitcast_convert_fusion
  135.7 0.1 convert_reduce_fusion.1
  135.8 0.5 slice_bitcast_fusion
  (22 shorter events, 0.2 us)
Async XLA Ops:
  0.6 16.8 %copy-start = (bf16[5376,128]{1,0:T(8,128)(2,1)S(1)}, bf16[5376,128]{1,0:T(8,128)(2,1)}, u32[]{:S(2)}) copy-start(bf16[5376,128]{1,0:T(8,128)(2,1)} %param.10) | copy-start | bytes 4128772
  3.7 38.2 %all-to-all-start = ((bf16[64,2,24,128]{3,2,1,0:T(8,128)(2,1)}), bf16[64,2,24,128]{3,2,1,0:T(8,128)(2,1)S(1)}, u32[]{:S(2)}, u32[]{:S(2)}) async-start(bf16[64,2,24,128]{3,2,1,0:T(8,128)(2,1)} %shard_map.137), calls=%async_computation | async-start | bytes 1572864 | tf_op jit(solution)/shard_map/all_to_all | solution.py:465
  17.4 0.7 copy-start.9
  17.4 0.7 copy-start.10
  17.4 0.7 copy-start.11
  17.6 1.1 copy-start.5
  17.6 1.1 copy-start.7
  18.8 3.5 %copy-start.8 = (bf16[1024,128]{1,0:T(8,128)(2,1)S(1)}, bf16[1024,128]{1,0:T(8,128)(2,1)}, u32[]{:S(2)}) copy-start(bf16[1024,128]{1,0:T(8,128)(2,1)} %param.11) | copy-start | bytes 786436
  18.8 23.2 %copy-start.4 = (s32[8,1536]{1,0:T(8,128)S(1)}, s32[8,1536]{1,0:T(8,128)}, u32[]{:S(2)}) copy-start(s32[8,1536]{1,0:T(8,128)} %constant.74.clone.lane_ref) | copy-start | bytes 147460
  19.8 32.9 %collective-permute-start = (bf16[3728,128]{1,0:T(8,128)(2,1)}, bf16[3728,128]{1,0:T(8,128)(2,1)S(1)}, u32[]{:S(2)}, u32[]{:S(2)}) collective-permute-start(bf16[3728,128]{1,0:T(8,128)(2,1)} %pad_maximum_fusion.4), channel_id=1, source_target_pairs={{0,2},{2,0},{1,3},{3,1},{4,6},{6,4},{5,7},{7,5},{8,10},{10,8},{9,1... | collective-permute-start | bytes 2863112 | tf_op jit(solution)/shard_map/ppermute | solution.py:38
  44.8 32.3 %all-to-all-start.1 = ((bf16[128,24,128]{2,1,0:T(8,128)(2,1)}), bf16[128,24,128]{2,1,0:T(8,128)(2,1)S(1)}, u32[]{:S(2)}, u32[]{:S(2)}) async-start(bf16[128,24,128]{2,1,0:T(8,128)(2,1)} %bitcast.1), calls=%async_computation.1 | async-start | bytes 1572864 | tf_op jit(solution)/shard_map/all_to_all | solution.py:467
  52.6 1.4 %copy-start.6 = (bf16[1,2384,128]{2,1,0:T(8,128)(2,1)S(1)}, bf16[1,2384,128]{2,1,0:T(8,128)(2,1)}, u32[]{:S(2)}) copy-start(bf16[1,2384,128]{2,1,0:T(8,128)(2,1)} %maximum_bitcast_fusion) | copy-start | bytes 1830916
  52.7 1.5 %copy-start.1 = (bf16[3728,128]{1,0:T(8,128)(2,1)}, bf16[3728,128]{1,0:T(8,128)(2,1)S(1)}, u32[]{:S(2)}) copy-start(bf16[3728,128]{1,0:T(8,128)(2,1)S(1)} %collective-permute-done.link_ref) | copy-start | bytes 2863108
  54.1 3.1 %copy-start.3 = (s32[3]{0:T(128)S(1)}, s32[3]{0:T(128)}, u32[]{:S(2)}) copy-start(s32[3]{0:T(128)} %lengths_ref.1) | copy-start | bytes 40
  54.2 3.0 %collective-permute-start.1 = (bf16[2,2384,128]{2,1,0:T(8,128)(2,1)S(1)}, bf16[2,2384,128]{2,1,0:T(8,128)(2,1)S(1)}, u32[]{:S(2)}, u32[]{:S(2)}) collective-permute-start(bf16[2,2384,128]{2,1,0:T(8,128)(2,1)S(1)} %pad_maximum_fusion.3), channel_id=1, source_target_pairs={{0,1},{1,0},{2,3},{3,2},{4,5},{5,4},{6,7},{7,6},{8,9},{9,8},{10,11... | collective-permute-start | bytes 3661832 | tf_op jit(solution)/shard_map/ppermute | solution.py:38
  57.2 1.2 copy-start.2
  77.1 2.6 %collective-permute-start.2 = (bf16[32,2,24,128]{3,2,1,0:T(8,128)(2,1)S(1)}, bf16[32,2,24,128]{3,2,1,0:T(8,128)(2,1)S(1)}, u32[]{:S(2)}, u32[]{:S(2)}) collective-permute-start(bf16[32,2,24,128]{3,2,1,0:T(8,128)(2,1)S(1)} %dynamic-slice_bitcast_fusion), channel_id=1, source_target_pairs={{0,1},{1,0},{2,3},{3,2},{4,5},{5,4},{6,7},{7,6},{8,9},{9,8},{10,11... | collective-permute-start | bytes 1179656 | tf_op jit(solution)/shard_map/ppermute | solution.py:38
  82.0 2.3 %collective-permute-start.5 = (bf16[2,1040,128]{2,1,0:T(8,128)(2,1)S(1)}, bf16[2,1040,128]{2,1,0:T(8,128)(2,1)S(1)}, u32[]{:S(2)}, u32[]{:S(2)}) collective-permute-start(bf16[2,1040,128]{2,1,0:T(8,128)(2,1)S(1)} %get-tuple-element.40), channel_id=1, source_target_pairs={{0,1},{1,0},{2,3},{3,2},{4,5},{5,4},{6,7},{7,6},{8,9},{9,8},{10,11... | collective-permute-start | bytes 1597448 | tf_op jit(solution)/shard_map/ppermute | solution.py:38
  83.8 12.1 %collective-permute-start.3 = (bf16[2,2,768,128]{3,2,1,0:T(8,128)(2,1)S(1)}, bf16[2,2,768,128]{3,2,1,0:T(8,128)(2,1)S(1)}, u32[]{:S(2)}, u32[]{:S(2)}) collective-permute-start(bf16[2,2,768,128]{3,2,1,0:T(8,128)(2,1)S(1)} %get-tuple-element.38), channel_id=1, source_target_pairs={{0,1},{1,0},{2,3},{3,2},{4,5},{5,4},{6,7},{7,6},{8,9},{9,8},{10,11... | collective-permute-start | bytes 2359304 | tf_op jit(solution)/shard_map/ppermute | solution.py:38
  85.2 27.8 %all-to-all-start.2 = ((bf16[128,16,128]{2,1,0:T(8,128)(2,1)}), bf16[128,16,128]{2,1,0:T(8,128)(2,1)S(1)}, u32[]{:S(2)}, u32[]{:S(2)}) async-start(bf16[128,16,128]{2,1,0:T(8,128)(2,1)} %bitcast.26), calls=%async_computation.2 | async-start | bytes 1048576 | tf_op jit(solution)/shard_map/all_to_all | solution.py:524
  92.1 3.7 %collective-permute-start.6 = (f32[8,128]{1,0:T(8,128)S(1)}, f32[8,128]{1,0:T(8,128)S(1)}, u32[]{:S(2)}, u32[]{:S(2)}) collective-permute-start(f32[8,128]{1,0:T(8,128)S(1)} %dynamic-slice_bitcast_fusion.2), channel_id=1, source_target_pairs={{0,2},{2,0},{1,3},{3,1},{4,6},{6,4},{5,7},{7,5},{8,10},{10,8},{9,1... | collective-permute-start | bytes 12296 | tf_op jit(solution)/shard_map/ppermute | solution.py:38
  95.9 22.8 %collective-permute-start.4 = (bf16[2,2,768,128]{3,2,1,0:T(8,128)(2,1)S(1)}, bf16[2,2,768,128]{3,2,1,0:T(8,128)(2,1)}, u32[]{:S(2)}, u32[]{:S(2)}) collective-permute-start(bf16[2,2,768,128]{3,2,1,0:T(8,128)(2,1)S(1)} %fusion.2), channel_id=1, source_target_pairs={{0,2},{2,0},{1,3},{3,1},{4,6},{6,4},{5,7},{7,5},{8,10},{10,8},{9,1... | collective-permute-start | bytes 2359304 | tf_op jit(solution)/shard_map/ppermute | solution.py:38
  114.0 20.8 %all-to-all-start.3 = ((bf16[64,24,128]{2,1,0:T(8,128)(2,1)}), bf16[64,24,128]{2,1,0:T(8,128)(2,1)S(1)}, u32[]{:S(2)}, u32[]{:S(2)}) async-start(bf16[64,24,128]{2,1,0:T(8,128)(2,1)} %broadcast_in_dim.7), calls=%async_computation.3 | async-start | bytes 786432 | tf_op jit(solution)/shard_map/all_to_all | solution.py:532

commit v3 on v2

--- a/solution.py
+++ b/solution.py
@@ -213,9 +213,12 @@
         here = valid - (index % BPU) * BLOCK - (link * 2 + core) * FRAMES
         limit = jnp.where(slot == index, here, limit)
     limits = jnp.concatenate([limit - frame for frame in range(frames)], axis=0)
-    slope_ref[:, :channels] = jnp.where(limits > step * frames, slope, 0.0)
-    slope_ref[:, channels:] = jnp.broadcast_to(inv_spread, (rows, LANES))
-    normed_ref[...] = normed
+    slope_ref[:, :channels] = jnp.where(limits > step * frames, slope, 0.0).astype(jnp.bfloat16)
+    inv_high = inv_spread.astype(jnp.bfloat16).astype(jnp.float32)
+    lower_half = lax.broadcasted_iota(jnp.int32, (rows, LANES), 1) < LANES // 2
+    inv_terms = jnp.where(lower_half, inv_high, inv_spread - inv_high)
+    slope_ref[:, channels:] = inv_terms.astype(jnp.bfloat16)
+    normed_ref[...] = normed.astype(jnp.bfloat16)
 
 
 def forward(link, core, lengths, feats, packed, from_link, from_core):
@@ -250,8 +253,8 @@
         ),
         out_shape=(
             pltpu.HBM((2 * channels, rows), jnp.bfloat16),
-            pltpu.HBM((rows, channels + LANES), jnp.float32),
-            pltpu.HBM((rows, channels), jnp.float32),
+            pltpu.HBM((rows, channels + LANES), jnp.bfloat16),
+            pltpu.HBM((rows, channels), jnp.bfloat16),
             jax.ShapeDtypeStruct((packed.shape[0], channels), jnp.bfloat16),
         ),
         compiler_params=pltpu.CompilerParams(vmem_limit_bytes=VMEM),
@@ -308,15 +311,17 @@
         columns.append(jnp.where(first, own, other))
         columns.append(jnp.where(first, other, own))
     upstream = jnp.concatenate(columns, axis=1)
-    normed = normed_ref[...]
+    normed = normed_ref[...].astype(jnp.float32)
     channels = normed.shape[1]
-    grad_act = upstream * slope_ref[:, :channels]
+    grad_act = upstream * slope_ref[:, :channels].astype(jnp.float32)
+    inv_terms = slope_ref[:, channels:].astype(jnp.float32)
+    inv_spread = inv_terms[:, :1] + inv_terms[:, LANES // 2 : LANES // 2 + 1]
     weighted = grad_act * normed
     gain = parameter(gain_ref[...], 1)
     grad_normed = grad_act * gain
     grad_mean = jnp.sum(grad_normed, axis=1, keepdims=True) * (1.0 / channels)
     cross_mean = jnp.sum(weighted * gain, axis=1, keepdims=True) * (1.0 / channels)
-    grad_pre = slope_ref[:, channels : channels + 1] * (grad_normed - grad_mean - normed * cross_mean)
+    grad_pre = inv_spread * (grad_normed - grad_mean - normed * cross_mean)
     low_ref[here, :] = grad_pre.astype(jnp.bfloat16)
     sums = jnp.concatenate(
         [

time: 137 us -> 137 us (level)
  no operation moved by 1% of the time
where the time goes in v3:
time: 137 us; the launch traced here: 136 us
  waiting for transfers between devices  65.8 us (48%)
  starting transfers between devices  37.8 us (28%)
  Pallas kernels  17.7 us (13%)
  local copies, waits for them, and re-layouts  8.77 us (6%)
  other arithmetic  5.06 us (4%)
    all_to_all x1, waiting for transfers between devices, route(): lax.all_to_all(outgoing, 'dp', split_axis=0, concat_axis=0, tiled=True)  18.9 us
    all_to_all x1, waiting for transfers between devices, on_device(): lax.all_to_all(chip_weight.reshape(2 * DP, 16, LANES), ('dp', 'l'), split...  16 us
    all_to_all x1, starting transfers between devices, route(): lax.all_to_all(outgoing, 'dp', split_axis=0, concat_axis=0, tiled=True)  13.7 us
    all_to_all x1, waiting for transfers between devices, route(): lax.all_to_all(sorted_pieces, ('dp', 'l'), split_axis=0, concat_axis=0, t...  13.3 us
    all_to_all x1, waiting for transfers between devices, on_device(): lax.all_to_all(jnp.broadcast_to(announce, (DP, PAD, LANES)), 'dp', split_...  12 us
    all_to_all x1, starting transfers between devices, route(): lax.all_to_all(sorted_pieces, ('dp', 'l'), split_axis=0, concat_axis=0, t...  7.87 us
    all_to_all x1, starting transfers between devices, on_device(): lax.all_to_all(chip_weight.reshape(2 * DP, 16, LANES), ('dp', 'l'), split...  6.93 us
    ppermute x7, waiting for transfers between devices, swap(): return lax.ppermute(value, axis, [(0, 1), (1, 0)])  5.76 us
  transfers between devices with their start and end apart: 11, of which 7 were waited for; matrix products, arithmetic and copies ran while one was open for 6% of the time, Pallas kernels for 9%

profile of v3, /device:TPU:2, one launch (start us, length us, event | category | flops | bytes accessed | tf_op | source)
XLA Modules:
  0.0 136.1 jit_solution(14235918150165173450)
XLA Ops:
  0.6 0.0 copy-start
  0.6 3.1 %shard_map.137 = bf16[64,2,24,128]{3,2,1,0:T(8,128)(2,1)} custom-call(bf16[2688,128]{1,0:T(8,128)(2,1)} %rows_ref.1, s32[21]{0:T(128)} %owner_ref.1, s32[21]{0:T(128)} %slot_ref.1), custom_call_target="tpu_custom_call" | custom-call | bytes 1500000 | tf_op jit(solution)/shard_map/pallas_call | solution.py:79
  3.7 13.7 %all-to-all-start = ((bf16[64,2,24,128]{3,2,1,0:T(8,128)(2,1)}), bf16[64,2,24,128]{3,2,1,0:T(8,128)(2,1)S(1)}, u32[]{:S(2)}, u32[]{:S(2)}) async-start(bf16[64,2,24,128]{3,2,1,0:T(8,128)(2,1)} %shard_map.137), calls=%async_computation | async-start | bytes 1572864 | tf_op jit(solution)/shard_map/all_to_all | solution.py:470
  17.4 0.0 copy-start.9
  17.4 0.0 copy-start.10
  17.4 0.0 copy-start.11
  17.5 0.0 copy-done
  17.5 0.1 copy.17
  17.6 0.0 copy-start.5
  17.6 0.0 copy-start.7
  17.6 0.4 copy-done.9
  18.1 0.0 copy-done.10
  18.1 0.0 copy-done.11
  18.1 0.1 constant_dynamic-slice_fusion.1
  18.2 0.5 copy-done.5
  18.7 0.1 copy-done.7
  18.8 1.0 pad_maximum_fusion.4
  19.8 1.4 %collective-permute-start = (bf16[3728,128]{1,0:T(8,128)(2,1)}, bf16[3728,128]{1,0:T(8,128)(2,1)S(1)}, u32[]{:S(2)}, u32[]{:S(2)}) collective-permute-start(bf16[3728,128]{1,0:T(8,128)(2,1)} %pad_maximum_fusion.4), channel_id=1, source_target_pairs={{0,2},{2,0},{1,3},{3,1},{4,6},{6,4},{5,7},{7,5},{8,10},{10,8},{9,1... | collective-permute-start | bytes 2863112 | tf_op jit(solution)/shard_map/ppermute | solution.py:38
  21.2 1.0 dynamic-slice_bitcast_fusion.1
  22.2 0.9 maximum_bitcast_fusion
  23.1 18.9 %all-to-all-done.spread_ref = bf16[64,2,24,128]{3,2,1,0:T(8,128)(2,1)S(1)} async-done(((bf16[64,2,24,128]{3,2,1,0:T(8,128)(2,1)}), bf16[64,2,24,128]{3,2,1,0:T(8,128)(2,1)S(1)}, u32[]{:S(2)}, u32[]{:S(2)}) %all-to-all-start) | async-done | bytes 786464 | tf_op jit(solution)/shard_map/all_to_all | solution.py:470
  42.0 2.8 %shard_map.138 = bf16[64,2,24,128]{3,2,1,0:T(8,128)(2,1)} custom-call(s32[8,1536]{1,0:T(8,128)S(1)} %copy-done.4, bf16[64,2,24,128]{3,2,1,0:T(8,128)(2,1)S(1)} %all-to-all-done.spread_ref), custom_call_target="tpu_custom_call" | custom-call | flops 4831838208 | bytes 1600000 | tf_op jit(solution)/shard_map/pallas_call | solution.py:134
  44.8 7.9 %all-to-all-start.1 = ((bf16[128,24,128]{2,1,0:T(8,128)(2,1)}), bf16[128,24,128]{2,1,0:T(8,128)(2,1)S(1)}, u32[]{:S(2)}, u32[]{:S(2)}) async-start(bf16[128,24,128]{2,1,0:T(8,128)(2,1)} %bitcast.1), calls=%async_computation.1 | async-start | bytes 1572864 | tf_op jit(solution)/shard_map/all_to_all | solution.py:472
  52.7 0.0 collective-permute-done.link_ref
  52.7 0.0 copy-start.1
  52.8 1.3 copy-done.6
  54.1 0.1 pad_maximum_fusion.3
  54.2 0.0 copy-done.1
  54.2 0.1 collective-permute-start.1
  54.3 0.1 pad_add_fusion.place_ref
  54.4 2.8 %collective-permute-done.1.beside_ref = bf16[2,2384,128]{2,1,0:T(8,128)(2,1)S(1)} collective-permute-done((bf16[2,2384,128]{2,1,0:T(8,128)(2,1)S(1)}, bf16[2,2384,128]{2,1,0:T(8,128)(2,1)S(1)}, u32[]{:S(2)}, u32[]{:S(2)}) %collective-permute-start.1) | collective-permute-done | bytes 1220640 | tf_op jit(solution)/shard_map/ppermute | solution.py:38
  57.2 1.2 copy-done.2
  58.4 5.4 %shard_map.139 = (bf16[1024,768]{1,0:T(8,128)(2,1)}, bf16[768,640]{1,0:T(8,128)(2,1)}, bf16[768,512]{1,0:T(8,128)(2,1)}, bf16[1040,512]{1,0:T(8,128)(2,1)S(1)}) custom-call(s32[2]{0:T(128)S(1)} %pad_add_fusion.place_ref, s32[3]{0:T(128)S(1)} %copy-done.3, bf16[21,4,64,128]{3,2,1,0:T(8,128)(2,1)S(1)} %bitcast.57, ...), custom_call_target="tpu_custom_call" | custom-call | flops 2415919104 | bytes 8000000 | tf_op jit(solution)/shard_map/pallas_call | solution.py:229
  63.8 13.3 %all-to-all-done.1 = bf16[128,24,128]{2,1,0:T(8,128)(2,1)S(1)} async-done(((bf16[128,24,128]{2,1,0:T(8,128)(2,1)}), bf16[128,24,128]{2,1,0:T(8,128)(2,1)S(1)}, u32[]{:S(2)}, u32[]{:S(2)}) %all-to-all-start.1) | async-done | bytes 786464 | tf_op jit(solution)/shard_map/all_to_all | solution.py:472
  77.1 0.1 collective-permute-start.2
  77.2 2.1 %shard_map.140 = (bf16[768,640]{1,0:T(8,128)(2,1)S(1)}, bf16[768,512]{1,0:T(8,128)(2,1)S(1)}, bf16[1024,768]{1,0:T(8,128)(2,1)S(1)}) custom-call(bf16[768,640]{1,0:T(8,128)(2,1)} %get-tuple-element.29.slope_hbm, bf16[768,512]{1,0:T(8,128)(2,1)} %get-tuple-element.30.normed_hbm, bf16[1024,768]{1,0:T(8,128)(2,1)} %get-tuple-element.31.transposed_hbm), custom_call_target="tpu_custom_call" | custom-call | bytes 10000000 | tf_op jit(solution)/shard_map/pallas_call | solution.py:288
  79.4 0.0 collective-permute-done.2.other_ref
  79.4 2.4 %shard_map.141 = (bf16[768,512]{1,0:T(8,128)(2,1)S(1)}, f32[2,1032,128]{2,1,0:T(8,128)S(1)}, bf16[2,1040,128]{2,1,0:T(8,128)(2,1)S(1)}) custom-call(s32[1]{0:T(128)} %bitcast.core_ref, bf16[2,32,2,24,128]{4,3,2,1,0:T(8,128)(2,1)S(1)} %bitcast.53, bf16[32,2,24,128]{3,2,1,0:T(8,128)(2,1)S(1)} %collective-permute-done.2.other_ref, ...), custom_call_target="tpu_custom_call" | custom-call | flops 805306368 | bytes 9000000 | tf_op jit(solution)/shard_map/pallas_call | solution.py:371
  81.8 0.8 collective-permute-start.5
  82.5 1.0 shard_map.142
  83.6 0.1 collective-permute-start.3
  83.7 0.4 collective-permute-done.5.other_ref
  84.1 0.9 shard_map.143
  84.9 6.9 %all-to-all-start.2 = ((bf16[128,16,128]{2,1,0:T(8,128)(2,1)}), bf16[128,16,128]{2,1,0:T(8,128)(2,1)S(1)}, u32[]{:S(2)}, u32[]{:S(2)}) async-start(bf16[128,16,128]{2,1,0:T(8,128)(2,1)} %bitcast.26), calls=%async_computation.2 | async-start | bytes 1048576 | tf_op jit(solution)/shard_map/all_to_all | solution.py:529
  91.9 1.1 collective-permute-start.6
  93.0 0.1 pad.8.clone
  93.1 2.5 %collective-permute-done.6 = f32[8,128]{1,0:T(8,128)S(1)} collective-permute-done((f32[8,128]{1,0:T(8,128)S(1)}, f32[8,128]{1,0:T(8,128)S(1)}, u32[]{:S(2)}, u32[]{:S(2)}) %collective-permute-start.6) | collective-permute-done | bytes 4128 | tf_op jit(solution)/shard_map/ppermute | solution.py:38
  95.6 0.0 collective-permute-done.3
  95.6 0.1 fusion.2
  95.7 1.1 collective-permute-start.4
  96.8 16.0 %all-to-all-done.2 = bf16[128,16,128]{2,1,0:T(8,128)(2,1)S(1)} async-done(((bf16[128,16,128]{2,1,0:T(8,128)(2,1)}), bf16[128,16,128]{2,1,0:T(8,128)(2,1)S(1)}, u32[]{:S(2)}, u32[]{:S(2)}) %all-to-all-start.2) | async-done | bytes 524320 | tf_op jit(solution)/shard_map/all_to_all | solution.py:529
  112.8 0.1 convert_reduce_fusion
  112.9 0.1 maximum_maximum_fusion
  113.0 0.8 broadcast_in_dim.7
  113.8 4.6 %all-to-all-start.3 = ((bf16[64,24,128]{2,1,0:T(8,128)(2,1)}), bf16[64,24,128]{2,1,0:T(8,128)(2,1)S(1)}, u32[]{:S(2)}, u32[]{:S(2)}) async-start(bf16[64,24,128]{2,1,0:T(8,128)(2,1)} %broadcast_in_dim.7), calls=%async_computation.3 | async-start | bytes 786432 | tf_op jit(solution)/shard_map/all_to_all | solution.py:537
  118.5 0.0 collective-permute-done.4
  118.5 1.2 broadcast_select_fusion.1
  119.7 0.2 broadcast_select_fusion.3
  119.9 0.3 fusion
  120.2 2.5 %copy.18 = bf16[21,4,32,2,128]{4,3,2,1,0:T(2,128)(2,1)} copy(bf16[21,4,32,2,128]{4,0,2,3,1:T(8,128)(2,1)S(1)} %fusion) | data formatting | bytes 2752512 | tf_op jit(solution)/shard_map/transpose | solution.py:555
  122.7 12.0 %all-to-all-done.3 = bf16[64,24,128]{2,1,0:T(8,128)(2,1)S(1)} async-done(((bf16[64,24,128]{2,1,0:T(8,128)(2,1)}), bf16[64,24,128]{2,1,0:T(8,128)(2,1)S(1)}, u32[]{:S(2)}, u32[]{:S(2)}) %all-to-all-start.3) | async-done | bytes 393248 | tf_op jit(solution)/shard_map/all_to_all | solution.py:537
  134.7 0.8 bitcast_convert_fusion
  135.5 0.1 convert_reduce_fusion.1
  135.6 0.5 slice_bitcast_fusion
  (22 shorter events, 0.2 us)
Async XLA Ops:
  0.6 16.8 %copy-start = (bf16[5376,128]{1,0:T(8,128)(2,1)S(1)}, bf16[5376,128]{1,0:T(8,128)(2,1)}, u32[]{:S(2)}) copy-start(bf16[5376,128]{1,0:T(8,128)(2,1)} %param.10) | copy-start | bytes 4128772
  3.7 38.2 %all-to-all-start = ((bf16[64,2,24,128]{3,2,1,0:T(8,128)(2,1)}), bf16[64,2,24,128]{3,2,1,0:T(8,128)(2,1)S(1)}, u32[]{:S(2)}, u32[]{:S(2)}) async-start(bf16[64,2,24,128]{3,2,1,0:T(8,128)(2,1)} %shard_map.137), calls=%async_computation | async-start | bytes 1572864 | tf_op jit(solution)/shard_map/all_to_all | solution.py:470
  17.4 0.7 copy-start.9
  17.4 0.7 copy-start.10
  17.4 0.7 copy-start.11
  17.6 1.1 copy-start.5
  17.6 1.1 copy-start.7
  18.8 3.5 %copy-start.8 = (bf16[1024,128]{1,0:T(8,128)(2,1)S(1)}, bf16[1024,128]{1,0:T(8,128)(2,1)}, u32[]{:S(2)}) copy-start(bf16[1024,128]{1,0:T(8,128)(2,1)} %param.11) | copy-start | bytes 786436
  18.8 23.2 %copy-start.4 = (s32[8,1536]{1,0:T(8,128)S(1)}, s32[8,1536]{1,0:T(8,128)}, u32[]{:S(2)}) copy-start(s32[8,1536]{1,0:T(8,128)} %constant.74.clone.lane_ref) | copy-start | bytes 147460
  19.8 32.9 %collective-permute-start = (bf16[3728,128]{1,0:T(8,128)(2,1)}, bf16[3728,128]{1,0:T(8,128)(2,1)S(1)}, u32[]{:S(2)}, u32[]{:S(2)}) collective-permute-start(bf16[3728,128]{1,0:T(8,128)(2,1)} %pad_maximum_fusion.4), channel_id=1, source_target_pairs={{0,2},{2,0},{1,3},{3,1},{4,6},{6,4},{5,7},{7,5},{8,10},{10,8},{9,1... | collective-permute-start | bytes 2863112 | tf_op jit(solution)/shard_map/ppermute | solution.py:38
  44.8 32.3 %all-to-all-start.1 = ((bf16[128,24,128]{2,1,0:T(8,128)(2,1)}), bf16[128,24,128]{2,1,0:T(8,128)(2,1)S(1)}, u32[]{:S(2)}, u32[]{:S(2)}) async-start(bf16[128,24,128]{2,1,0:T(8,128)(2,1)} %bitcast.1), calls=%async_computation.1 | async-start | bytes 1572864 | tf_op jit(solution)/shard_map/all_to_all | solution.py:472
  52.6 1.4 %copy-start.6 = (bf16[1,2384,128]{2,1,0:T(8,128)(2,1)S(1)}, bf16[1,2384,128]{2,1,0:T(8,128)(2,1)}, u32[]{:S(2)}) copy-start(bf16[1,2384,128]{2,1,0:T(8,128)(2,1)} %maximum_bitcast_fusion) | copy-start | bytes 1830916
  52.7 1.5 %copy-start.1 = (bf16[3728,128]{1,0:T(8,128)(2,1)}, bf16[3728,128]{1,0:T(8,128)(2,1)S(1)}, u32[]{:S(2)}) copy-start(bf16[3728,128]{1,0:T(8,128)(2,1)S(1)} %collective-permute-done.link_ref) | copy-start | bytes 2863108
  54.1 3.1 %copy-start.3 = (s32[3]{0:T(128)S(1)}, s32[3]{0:T(128)}, u32[]{:S(2)}) copy-start(s32[3]{0:T(128)} %lengths_ref.1) | copy-start | bytes 40
  54.2 3.0 %collective-permute-start.1 = (bf16[2,2384,128]{2,1,0:T(8,128)(2,1)S(1)}, bf16[2,2384,128]{2,1,0:T(8,128)(2,1)S(1)}, u32[]{:S(2)}, u32[]{:S(2)}) collective-permute-start(bf16[2,2384,128]{2,1,0:T(8,128)(2,1)S(1)} %pad_maximum_fusion.3), channel_id=1, source_target_pairs={{0,1},{1,0},{2,3},{3,2},{4,5},{5,4},{6,7},{7,6},{8,9},{9,8},{10,11... | collective-permute-start | bytes 3661832 | tf_op jit(solution)/shard_map/ppermute | solution.py:38
  57.2 1.2 copy-start.2
  77.1 2.2 %collective-permute-start.2 = (bf16[32,2,24,128]{3,2,1,0:T(8,128)(2,1)S(1)}, bf16[32,2,24,128]{3,2,1,0:T(8,128)(2,1)S(1)}, u32[]{:S(2)}, u32[]{:S(2)}) collective-permute-start(bf16[32,2,24,128]{3,2,1,0:T(8,128)(2,1)S(1)} %dynamic-slice_bitcast_fusion), channel_id=1, source_target_pairs={{0,1},{1,0},{2,3},{3,2},{4,5},{5,4},{6,7},{7,6},{8,9},{9,8},{10,11... | collective-permute-start | bytes 1179656 | tf_op jit(solution)/shard_map/ppermute | solution.py:38
  81.8 2.3 %collective-permute-start.5 = (bf16[2,1040,128]{2,1,0:T(8,128)(2,1)S(1)}, bf16[2,1040,128]{2,1,0:T(8,128)(2,1)S(1)}, u32[]{:S(2)}, u32[]{:S(2)}) collective-permute-start(bf16[2,1040,128]{2,1,0:T(8,128)(2,1)S(1)} %get-tuple-element.40), channel_id=1, source_target_pairs={{0,1},{1,0},{2,3},{3,2},{4,5},{5,4},{6,7},{7,6},{8,9},{9,8},{10,11... | collective-permute-start | bytes 1597448 | tf_op jit(solution)/shard_map/ppermute | solution.py:38
  83.6 12.1 %collective-permute-start.3 = (bf16[2,2,768,128]{3,2,1,0:T(8,128)(2,1)S(1)}, bf16[2,2,768,128]{3,2,1,0:T(8,128)(2,1)S(1)}, u32[]{:S(2)}, u32[]{:S(2)}) collective-permute-start(bf16[2,2,768,128]{3,2,1,0:T(8,128)(2,1)S(1)} %get-tuple-element.38), channel_id=1, source_target_pairs={{0,1},{1,0},{2,3},{3,2},{4,5},{5,4},{6,7},{7,6},{8,9},{9,8},{10,11... | collective-permute-start | bytes 2359304 | tf_op jit(solution)/shard_map/ppermute | solution.py:38
  84.9 27.8 %all-to-all-start.2 = ((bf16[128,16,128]{2,1,0:T(8,128)(2,1)}), bf16[128,16,128]{2,1,0:T(8,128)(2,1)S(1)}, u32[]{:S(2)}, u32[]{:S(2)}) async-start(bf16[128,16,128]{2,1,0:T(8,128)(2,1)} %bitcast.26), calls=%async_computation.2 | async-start | bytes 1048576 | tf_op jit(solution)/shard_map/all_to_all | solution.py:529
  91.9 3.7 %collective-permute-start.6 = (f32[8,128]{1,0:T(8,128)S(1)}, f32[8,128]{1,0:T(8,128)S(1)}, u32[]{:S(2)}, u32[]{:S(2)}) collective-permute-start(f32[8,128]{1,0:T(8,128)S(1)} %dynamic-slice_bitcast_fusion.2), channel_id=1, source_target_pairs={{0,2},{2,0},{1,3},{3,1},{4,6},{6,4},{5,7},{7,5},{8,10},{10,8},{9,1... | collective-permute-start | bytes 12296 | tf_op jit(solution)/shard_map/ppermute | solution.py:38
  95.7 22.8 %collective-permute-start.4 = (bf16[2,2,768,128]{3,2,1,0:T(8,128)(2,1)S(1)}, bf16[2,2,768,128]{3,2,1,0:T(8,128)(2,1)}, u32[]{:S(2)}, u32[]{:S(2)}) collective-permute-start(bf16[2,2,768,128]{3,2,1,0:T(8,128)(2,1)S(1)} %fusion.2), channel_id=1, source_target_pairs={{0,2},{2,0},{1,3},{3,1},{4,6},{6,4},{5,7},{7,5},{8,10},{10,8},{9,1... | collective-permute-start | bytes 2359304 | tf_op jit(solution)/shard_map/ppermute | solution.py:38
  113.8 20.8 %all-to-all-start.3 = ((bf16[64,24,128]{2,1,0:T(8,128)(2,1)}), bf16[64,24,128]{2,1,0:T(8,128)(2,1)S(1)}, u32[]{:S(2)}, u32[]{:S(2)}) async-start(bf16[64,24,128]{2,1,0:T(8,128)(2,1)} %broadcast_in_dim.7), calls=%async_computation.3 | async-start | bytes 786432 | tf_op jit(solution)/shard_map/all_to_all | solution.py:537
